TPU v7x, 512 devices: a whole 4x4x16 slice. The times are simulated.
512 devices in a mesh: head: 8 (over y, x_lo), outer: 16 (over z), inner: 4 (over x_hi, core).
Axes of the slice: x: 4 (x_hi: 2, x_lo: 2; x = x_hi * 2 + x_lo), y: 4, z: 16, core: 2. Of those that a mesh axis runs over, the one named last changes fastest.
Arguments:
- queries: bfloat16 [4096, 8192], P('outer', ('head', 'inner')), may hold values from -100 to 100
- keys: bfloat16 [4096, 1024], P('outer', 'head'), may hold values from -5 to 5
- values: bfloat16 [4096, 1024], P('outer', 'head'), may hold values from -6 to 6
- grad_out: bfloat16 [4096, 8192], P('outer', ('head', 'inner')), may hold values from -24 to 24
- hidden_in: bfloat16 [4096, 8192], P('outer', ('head', 'inner')), may hold values from -6 to 6
- adapter_a: bfloat16 [8192, 16], P(('head', 'inner')), may hold values from -0.0625 to 0.0625
- adapter_b: bfloat16 [16, 1024], P(None, 'head'), may hold values from -1.5 to 1.5
- block_order: int32 [32], replicated, may hold values from 0 to 31, each once
- doc_ids: int32 [4096], replicated, may hold values from 0 to 3, never falling along the last dimension, each value on 1 to 2048 neighbouring positions
Outputs:
- grad_query: bfloat16 [4096, 8192], P('outer', ('head', 'inner'))
- grad_key: bfloat16 [4096, 1024], P('outer', 'head')
- grad_value: bfloat16 [4096, 1024], P('outer', 'head')
- grad_a: float32 [8192, 16], P(('head', 'inner'))
- grad_b: float32 [16, 1024], P(None, 'head')
Inputs may be any that keep to these rules, and one draw needn't show every extreme that they name: `block_order`: a permutation of the stored blocks. `doc_ids`: never falling along positions; each document has 1 to 2048 positions.
All inputs are finite; a program needn't handle non-finite values.
Results may differ from a plain program's by a relative error of at most 0.024.
Values may be sent and summed in bfloat16 or wider, within the bound.
No kernel may reach another device: no remote copies, remote signals or barrier semaphores. Data moves between devices by JAX's collectives and lax.ppermute only.
A program may use at most 64 MiB of HBM per device.

v0:
```python
import jax
import jax.numpy as jnp
from jax import lax
from jax.sharding import PartitionSpec as P

HEAD_DIM = 128


NEGATIVE = -1e30


def copy_for_each(value, axis):
    devices = lax.axis_size(axis)
    return lax.all_to_all(
        jnp.broadcast_to(value[None], (devices, *value.shape)), axis, 0, 0, tiled=True
    )


def taken_together(value, axis):
    return copy_for_each(value, axis).sum(axis=0)


def in_one_piece(arrays, axis, dim, along):
    both = jnp.concatenate(arrays, axis=along)
    result, at, done = (lax.all_gather(both, axis, axis=dim, tiled=True), 0, [])
    for a in arrays:
        done.append(lax.slice_in_dim(result, at, at + a.shape[along], axis=along))
        at += a.shape[along]
    return tuple(done)


def in_one_piece_2(arrays, axis, dim, along):
    ends, at = ([], 0)
    for a in arrays[:-1]:
        at += a.shape[along]
        ends.append(at)
    both = jnp.concatenate(arrays, axis=along)
    return tuple(
        jnp.split(lax.psum_scatter(both, axis, scatter_dimension=dim, tiled=True), ends, axis=along)
    )


def taken_together_2(value, axis):
    everything = copy_for_each(value, axis)
    return jnp.sum(everything.astype(jnp.float32), axis=0)


def packed_total(arrays, axis):
    flat, at, done = (jnp.concatenate([a.reshape(-1) for a in arrays]), 0, [])
    running = taken_together(flat, axis)
    for a in arrays:
        done.append(running[at : at + a.size].reshape(a.shape))
        at += a.size
    return tuple(done)


def block_meta(block_table, doc_table, block_id, half_rows):
    first_pos = block_table[block_id] * half_rows
    places = first_pos + jnp.arange(half_rows, dtype=jnp.int32)
    owners = lax.dynamic_slice_in_dim(doc_table, first_pos, half_rows, 0)
    return (places, owners)


def joined_meta(first, second):
    return (jnp.concatenate((first[0], second[0]), 0), jnp.concatenate((first[1], second[1]), 0))


def visible(query_meta, key_meta):
    return (key_meta[0][None, :] <= query_meta[0][:, None]) & (
        key_meta[1][None, :] == query_meta[1][:, None]
    )


def tile_scores(query_tile, key_rows, scaling):
    return (
        jnp.einsum("tkgd,skd->kgts", query_tile, key_rows, preferred_element_type=jnp.float32)
        * scaling
    )


def forward_tile(carried, masked, query_tile, key_tile, value_tile, scaling):
    peak_score, totals, summed = carried
    kv_local = query_tile.shape[1]
    key_rows = key_tile.reshape(key_tile.shape[0], kv_local, -1)
    value_rows = value_tile.reshape(value_tile.shape[0], kv_local, -1)
    scores = jnp.where(masked, tile_scores(query_tile, key_rows, scaling), NEGATIVE)
    new_peak = jnp.maximum(peak_score, jnp.max(scores, axis=-1))
    weights = jnp.where(masked, jnp.exp(scores - new_peak[..., None]), 0.0)
    factor = jnp.exp(peak_score - new_peak)
    summed = summed * factor[..., None] + jnp.einsum(
        "kgts,skd->kgtd",
        weights.astype(jnp.bfloat16),
        value_rows,
        preferred_element_type=jnp.float32,
    )
    return (new_peak, totals * factor + jnp.sum(weights, axis=-1), summed)


def backward_tile(
    carried, masked, query_tile, grad_tile, lse_tile, delta_tile, key_tile, value_tile, scaling
):
    grad_query, grad_key, grad_value = carried
    kv_local = query_tile.shape[1]
    key_rows = key_tile.reshape(key_tile.shape[0], kv_local, -1)
    value_rows = value_tile.reshape(value_tile.shape[0], kv_local, -1)
    scores = tile_scores(query_tile, key_rows, scaling)
    prob_tile = jnp.where(masked, jnp.exp(scores - lse_tile[..., None]), 0.0)
    grad_value = jnp.einsum(
        "kgts,tkgd->skd",
        prob_tile.astype(jnp.bfloat16),
        grad_tile,
        preferred_element_type=jnp.float32,
    )
    dot_tile = jnp.einsum(
        "tkgd,skd->kgts", grad_tile, value_rows, preferred_element_type=jnp.float32
    )
    slopes = (prob_tile * (dot_tile - delta_tile[..., None])).astype(jnp.bfloat16)
    grad_query = grad_query + jnp.einsum(
        "kgts,skd->tkgd", slopes, key_rows, preferred_element_type=jnp.float32
    )
    grad_key = jnp.einsum("kgts,tkgd->skd", slopes, query_tile, preferred_element_type=jnp.float32)
    return (grad_query, grad_key, grad_value)


def on_device(
    queries, keys, values, grad_out, hidden_in, adapter_a, adapter_b, block_order, doc_ids
):
    member = lax.axis_index("outer")
    tokens = queries.shape[0]
    half_rows = tokens // 2
    kv_local = keys.shape[1] // HEAD_DIM
    grp_local = queries.shape[1] // (kv_local * HEAD_DIM)
    scaling = HEAD_DIM ** (-0.5)
    query_rows = queries.reshape(tokens, kv_local, grp_local, HEAD_DIM)
    grad_rows = grad_out.reshape(tokens, kv_local, grp_local, HEAD_DIM)
    own_meta = joined_meta(
        block_meta(block_order, doc_ids, 2 * member, half_rows),
        block_meta(block_order, doc_ids, 2 * member + 1, half_rows),
    )
    low_partial = jnp.dot(hidden_in, adapter_a, preferred_element_type=jnp.float32)
    low_rank = taken_together(low_partial, ("head", "inner")).astype(jnp.bfloat16)
    start_state = (
        jnp.full((kv_local, grp_local, tokens), NEGATIVE, jnp.float32),
        jnp.zeros((kv_local, grp_local, tokens), jnp.float32),
        jnp.zeros((kv_local, grp_local, tokens, HEAD_DIM), jnp.float32),
    )
    key_all, value_all = in_one_piece((keys, values), "outer", 0, 1)
    total_rows = key_all.shape[0]
    span = min(1024, total_rows)
    count = total_rows // span
    all_places = (
        block_order[:, None] * half_rows + jnp.arange(half_rows, dtype=jnp.int32)[None, :]
    ).reshape(-1)
    all_owners = jnp.take(doc_ids, all_places)
    pieces = (
        key_all.reshape(count, span, -1),
        value_all.reshape(count, span, -1),
        all_places.reshape(count, span),
        all_owners.reshape(count, span),
    )

    def forward_block(state, piece):
        masked = visible(own_meta, (piece[2], piece[3]))

        def forward_active(present):
            return forward_tile(present, masked, query_rows, piece[0], piece[1], scaling)

        def forward_resting(present):
            return present

        return (lax.cond(jnp.any(masked), forward_active, forward_resting, state), None)

    state, unused = lax.scan(forward_block, start_state, pieces)
    peak_score, totals, summed = state
    lse_rows = peak_score + jnp.log(totals)
    output = summed / totals[..., None]
    delta_rows = jnp.sum(
        output * jnp.transpose(grad_rows, (1, 2, 0, 3)).astype(jnp.float32), axis=-1
    )
    empty_query = jnp.zeros((tokens, kv_local, grp_local, HEAD_DIM), jnp.float32)
    empty_block = jnp.zeros((span, kv_local, HEAD_DIM), jnp.float32)

    def backward_block(grad_query, piece):
        masked = visible(own_meta, (piece[2], piece[3]))

        def backward_active(present):
            return backward_tile(
                present,
                masked,
                query_rows,
                grad_rows,
                lse_rows,
                delta_rows,
                piece[0],
                piece[1],
                scaling,
            )

        def backward_resting(present):
            return present

        grad_query, block_key, block_value = lax.cond(
            jnp.any(masked),
            backward_active,
            backward_resting,
            (grad_query, empty_block, empty_block),
        )
        return (grad_query, (block_key, block_value))

    grad_queries, (key_parts, value_parts) = lax.scan(backward_block, empty_query, pieces)
    key_full = key_parts.reshape(total_rows, kv_local, HEAD_DIM)
    value_full = value_parts.reshape(total_rows, kv_local, HEAD_DIM)
    key_acc, value_acc = tuple(
        (
            part.astype(jnp.float32)
            for part in in_one_piece_2(
                (key_full.astype(jnp.bfloat16), value_full.astype(jnp.bfloat16)), "outer", 0, 1
            )
        )
    )
    key_acc, value_acc = (
        taken_together_2(key_acc.astype(jnp.bfloat16), "inner").astype(jnp.float32),
        taken_together_2(value_acc.astype(jnp.bfloat16), "inner").astype(jnp.float32),
    )
    grad_query = (grad_queries * scaling).astype(jnp.bfloat16).reshape(tokens, -1)
    grad_key = (key_acc * scaling).astype(jnp.bfloat16).reshape(tokens, -1)
    grad_value = value_acc.astype(jnp.bfloat16).reshape(tokens, -1)
    back_partial = lax.dot_general(
        grad_key, adapter_b, (((1,), (1,)), ((), ())), preferred_element_type=jnp.float32
    )
    back_rank = taken_together(back_partial, "head").astype(jnp.bfloat16)
    grad_a_part = lax.dot_general(
        hidden_in, back_rank, (((0,), (0,)), ((), ())), preferred_element_type=jnp.float32
    )
    grad_b_part = lax.dot_general(
        low_rank, grad_key, (((0,), (0,)), ((), ())), preferred_element_type=jnp.float32
    )
    grad_a, grad_b = packed_total((grad_a_part, grad_b_part), "outer")
    return (grad_query, grad_key, grad_value, grad_a, grad_b)


def solution(mesh):
    in_specs = (
        P("outer", ("head", "inner")),
        P("outer", "head"),
        P("outer", "head"),
        P("outer", ("head", "inner")),
        P("outer", ("head", "inner")),
        P(("head", "inner"), None),
        P(None, "head"),
        P(),
        P(),
    )
    out_specs = (
        P("outer", ("head", "inner")),
        P("outer", "head"),
        P("outer", "head"),
        P(("head", "inner"), None),
        P(None, "head"),
    )
    return jax.shard_map(
        on_device, mesh=mesh, in_specs=in_specs, out_specs=out_specs, check_vma=False
    )
```

profile of v0, /device:TPU:2, one launch (start us, length us, event | category | flops | bytes accessed | tf_op | source)
XLA Modules:
  0.0 276.1 jit_solution(14876614145196556149)
XLA Ops:
  12.4 23.0 %gather_fusion = s32[4096]{0:T(1024)S(1)} fusion(s32[4096]{0:T(1024)S(1)} %copy-done.1, s32[4096]{0:T(1024)S(1)} %broadcast_clamp_fusion), kind=kCustom, calls=%fused_computation | custom fusion | bytes 49152 | tf_op jit(solution)/shard_map/jit(_take)/gather | solution.py:154
  36.2 52.3 %all-gather.2.cloned.1.call-done = bf16[4096,256]{1,0:T(8,128)(2,1)} async-done(((bf16[256,256]{1,0:T(8,128)(2,1)}), bf16[4096,256]{1,0:T(8,128)(2,1)}) %all-gather.2.cloned.1.call-update) | async-done | bytes 2097168 | tf_op jit(solution)/shard_map/all_gather | solution.py:25
  88.5 1.7 fusion.49
  90.2 16.0 %while.31 = (s32[]{:T(128)}, f32[1,2,256]{2,1,0:T(2,128)S(1)}, f32[1,2,256]{2,1,0:T(2,128)S(1)}, f32[1,2,256,128]{3,2,1,0:T(8,128)S(1)}, s32[4,1024]{1,0:T(4,128...) while((s32[]{:T(128)}, f32[1,2,256]{2,1,0:T(2,128)S(1)}, ...), condition=%wide.region_6.7_spmd, body=%wide.region_0.6_spmd.sunk | while | flops 276432384 | bytes 8579327 | solution.py:173
  92.2 2.0 conditional.4
  96.2 2.0 conditional.4
  100.2 2.0 conditional.4
  104.2 2.0 conditional.4
  106.4 20.5 %while.32 = (s32[]{:T(128)}, f32[256,1,2,128]{0,3,2,1:T(8,128)S(1)}, bf16[4,1024,1,128]{3,1,2,0:T(8,128)(2,1)}, bf16[4,1024,1,128]{3,1,2,0:T(8,128)(2,1)}, s32[4...) while((s32[]{:T(128)}, ...), condition=%wide.region_12.13_spmd, body=%wide.region_8.12_spmd.sunk | while | flops 675872768 | bytes 13400839 | solution.py:210
  108.4 2.3 conditional.5
  113.6 2.3 conditional.5
  118.6 2.3 conditional.5
  123.8 2.3 conditional.5
  126.9 3.1 %pad_maximum_fusion = bf16[4096,2,128]{2,0,1:T(8,128)(2,1)} fusion(bf16[4096,1,128]{2,0,1:T(8,128)(2,1)} %bitcast.179, bf16[4096,1,128]{2,0,1:T(8,128)(2,1)} %bitcast.178), kind=kLoop, calls=%fused_computation.63 | loop fusion | flops 1048576 | bytes 4194304 | tf_op jit(solution)/shard_map/concatenate | solution.py:37
  131.7 7.4 %all-to-all-start.3 = ((f32[32,256,16]{1,2,0:T(8,128)}), f32[32,256,16]{1,2,0:T(8,128)S(1)}, u32[]{:S(2)}, u32[]{:S(2)}) async-start(f32[32,256,16]{1,2,0:T(8,128)} %broadcast_in_dim.123), calls=%async_computation.4 | async-start | bytes 1048576 | tf_op jit(solution)/shard_map/all_to_all | solution.py:14
  139.1 59.3 %reduce-scatter.2.cloned.1.call-done = bf16[256,2,128]{2,0,1:T(8,128)(2,1)} async-done(((bf16[4096,2,128]{2,0,1:T(8,128)(2,1)}), bf16[256,2,128]{2,0,1:T(8,128)(2,1)}) %reduce-scatter.2.cloned.1.call-update) | async-done | bytes 131088 | tf_op jit(solution)/shard_map/reduce_scatter | solution.py:39
  200.1 3.4 %all-to-all-start = ((bf16[4,256,1,128]{3,1,2,0:T(8,128)(2,1)}), bf16[4,256,1,128]{3,1,2,0:T(8,128)(2,1)S(1)}, u32[]{:S(2)}, u32[]{:S(2)}) async-start(bf16[4,256,1,128]{3,1,2,0:T(8,128)(2,1)} %broadcast_in_dim.119), calls=%async_computation.1 | async-start | bytes 524288 | tf_op jit(solution)/shard_map/all_to_all | solution.py:14
  203.5 7.5 %all-to-all-done = bf16[4,256,1,128]{3,1,2,0:T(8,128)(2,1)S(1)} async-done(((bf16[4,256,1,128]{3,1,2,0:T(8,128)(2,1)}), bf16[4,256,1,128]{3,1,2,0:T(8,128)(2,1)S(1)}, u32[]{:S(2)}, u32[]{:S(2)}) %all-to-all-start) | async-done | bytes 262176 | tf_op jit(solution)/shard_map/all_to_all | solution.py:14
  211.9 5.7 %all-to-all-start.2 = ((f32[8,256,16]{1,2,0:T(8,128)}), f32[8,256,16]{1,2,0:T(8,128)S(1)}, u32[]{:S(2)}, u32[]{:S(2)}) async-start(f32[8,256,16]{1,2,0:T(8,128)} %broadcast_in_dim.122), calls=%async_computation.3 | async-start | bytes 262144 | tf_op jit(solution)/shard_map/all_to_all | solution.py:14
  217.7 5.3 %all-to-all-done.2 = f32[8,256,16]{1,2,0:T(8,128)S(1)} async-done(((f32[8,256,16]{1,2,0:T(8,128)}), f32[8,256,16]{1,2,0:T(8,128)S(1)}, u32[]{:S(2)}, u32[]{:S(2)}) %all-to-all-start.2) | async-done | bytes 131104 | tf_op jit(solution)/shard_map/all_to_all | solution.py:14
  223.7 3.4 %all-to-all-start.1 = ((bf16[4,256,1,128]{3,1,2,0:T(8,128)(2,1)}), bf16[4,256,1,128]{3,1,2,0:T(8,128)(2,1)S(1)}, u32[]{:S(2)}, u32[]{:S(2)}) async-start(bf16[4,256,1,128]{3,1,2,0:T(8,128)(2,1)} %broadcast_in_dim.121), calls=%async_computation.2 | async-start | bytes 524288 | tf_op jit(solution)/shard_map/all_to_all | solution.py:14
  227.5 7.1 %all-to-all-done.1 = bf16[4,256,1,128]{3,1,2,0:T(8,128)(2,1)S(1)} async-done(((bf16[4,256,1,128]{3,1,2,0:T(8,128)(2,1)}), bf16[4,256,1,128]{3,1,2,0:T(8,128)(2,1)S(1)}, u32[]{:S(2)}, u32[]{:S(2)}) %all-to-all-start.1) | async-done | bytes 262176 | tf_op jit(solution)/shard_map/all_to_all | solution.py:14
  235.6 8.8 %all-to-all-start.4 = ((f32[16,1,6144]{2,1,0:T(1,128)}), f32[16,1,6144]{2,1,0:T(1,128)S(1)}, u32[]{:S(2)}, u32[]{:S(2)}) async-start(f32[16,1,6144]{2,1,0:T(1,128)} %broadcast_in_dim.124), calls=%async_computation.5 | async-start | bytes 786432 | tf_op jit(solution)/shard_map/all_to_all | solution.py:14
  245.9 21.8 %all-to-all-done.4 = f32[16,1,6144]{2,1,0:T(1,128)S(1)} async-done(((f32[16,1,6144]{2,1,0:T(1,128)}), f32[16,1,6144]{2,1,0:T(1,128)S(1)}, u32[]{:S(2)}, u32[]{:S(2)}) %all-to-all-start.4) | async-done | bytes 393248 | tf_op jit(solution)/shard_map/all_to_all | solution.py:14
  (140 shorter events, 44.9 us)
Async XLA Ops:
  7.2 122.8 %copy-start = (bf16[256,256]{1,0:T(8,128)(2,1)S(1)}, bf16[256,256]{1,0:T(8,128)(2,1)}, u32[]{:S(2)}) copy-start(bf16[256,256]{1,0:T(8,128)(2,1)} %param.21) | copy-start | bytes 393220
  7.2 5.2 %copy-start.1 = (s32[4096]{0:T(1024)S(1)}, s32[4096]{0:T(1024)}, u32[]{:S(2)}) copy-start(s32[4096]{0:T(1024)} %param.25) | copy-start | bytes 49156
  7.2 81.3 %all-gather.2.cloned.1.call-start = ((), (), s32[]{:S(2)}) async-start(), calls=%async_computation.6 | async-start | bytes 2228224 | tf_op jit(solution)/shard_map/all_gather | solution.py:25
  8.8 189.6 %reduce-scatter.2.cloned.1.call-start = ((), (), s32[]{:S(2)}) async-start(), calls=%async_computation.7 | async-start | bytes 2228224 | tf_op jit(solution)/shard_map/reduce_scatter | solution.py:39
  12.4 23.1 %copy-start.3 = (bf16[256,256]{1,0:T(8,128)(2,1)S(1)}, bf16[256,256]{1,0:T(8,128)(2,1)}, u32[]{:S(2)}) copy-start(bf16[256,256]{1,0:T(8,128)(2,1)} %param.17) | copy-start | bytes 393220
  12.4 23.3 %copy-start.4 = (bf16[256,256]{1,0:T(8,128)(2,1)S(1)}, bf16[256,256]{1,0:T(8,128)(2,1)}, u32[]{:S(2)}) copy-start(bf16[256,256]{1,0:T(8,128)(2,1)} %param.20) | copy-start | bytes 393220
  130.0 0.7 copy-start.5
  130.7 80.4 %copy-start.6 = (bf16[16,128]{1,0:T(8,128)(2,1)S(1)}, bf16[16,128]{1,0:T(8,128)(2,1)}, u32[]{:S(2)}) copy-start(bf16[16,128]{1,0:T(8,128)(2,1)} %param.23) | copy-start | bytes 12292
  131.7 67.6 %all-to-all-start.3 = ((f32[32,256,16]{1,2,0:T(8,128)}), f32[32,256,16]{1,2,0:T(8,128)S(1)}, u32[]{:S(2)}, u32[]{:S(2)}) async-start(f32[32,256,16]{1,2,0:T(8,128)} %broadcast_in_dim.123), calls=%async_computation.4 | async-start | bytes 1048576 | tf_op jit(solution)/shard_map/all_to_all | solution.py:14
  200.1 10.9 %all-to-all-start = ((bf16[4,256,1,128]{3,1,2,0:T(8,128)(2,1)}), bf16[4,256,1,128]{3,1,2,0:T(8,128)(2,1)S(1)}, u32[]{:S(2)}, u32[]{:S(2)}) async-start(bf16[4,256,1,128]{3,1,2,0:T(8,128)(2,1)} %broadcast_in_dim.119), calls=%async_computation.1 | async-start | bytes 524288 | tf_op jit(solution)/shard_map/all_to_all | solution.py:14
  211.1 34.8 %copy-start.2 = (bf16[256,128]{1,0:T(8,128)(2,1)}, bf16[256,128]{1,0:T(8,128)(2,1)S(1)}, u32[]{:S(2)}) copy-start(bf16[256,128]{1,0:T(8,128)(2,1)S(1)} %multiply_convert_fusion.1) | copy-start | bytes 196612
  211.9 11.1 %all-to-all-start.2 = ((f32[8,256,16]{1,2,0:T(8,128)}), f32[8,256,16]{1,2,0:T(8,128)S(1)}, u32[]{:S(2)}, u32[]{:S(2)}) async-start(f32[8,256,16]{1,2,0:T(8,128)} %broadcast_in_dim.122), calls=%async_computation.3 | async-start | bytes 262144 | tf_op jit(solution)/shard_map/all_to_all | solution.py:14
  223.7 10.9 %all-to-all-start.1 = ((bf16[4,256,1,128]{3,1,2,0:T(8,128)(2,1)}), bf16[4,256,1,128]{3,1,2,0:T(8,128)(2,1)S(1)}, u32[]{:S(2)}, u32[]{:S(2)}) async-start(bf16[4,256,1,128]{3,1,2,0:T(8,128)(2,1)} %broadcast_in_dim.121), calls=%async_computation.2 | async-start | bytes 524288 | tf_op jit(solution)/shard_map/all_to_all | solution.py:14
  235.6 32.1 %all-to-all-start.4 = ((f32[16,1,6144]{2,1,0:T(1,128)}), f32[16,1,6144]{2,1,0:T(1,128)S(1)}, u32[]{:S(2)}, u32[]{:S(2)}) async-start(f32[16,1,6144]{2,1,0:T(1,128)} %broadcast_in_dim.124), calls=%async_computation.5 | async-start | bytes 786432 | tf_op jit(solution)/shard_map/all_to_all | solution.py:14
Sparse Core Ops, SparseCore 0:
  10.7 77.7 all-gather.1
  130.1 68.2 reduce-scatter.1
where the time goes:
time: 278 us; the launch traced here: 276 us
  waiting for transfers between devices  153 us (55%)
  local copies, waits for them, and re-layouts  38.3 us (14%)
  starting transfers between devices  28.8 us (10%)
  other arithmetic  19.3 us (7%)
  between operations  15.7 us (6%)
  matrix products  14.9 us (5%)
  loops' own time  5.8 us (2%)
    reduce_scatter x1, waiting for transfers between devices, in_one_piece_2(): lax.psum_scatter(both, axis, scatter_dimension=dim, tiled=True)  59.3 us
    all_gather x1, waiting for transfers between devices, in_one_piece(): result, at, done = (lax.all_gather(both, axis, axis=dim, tiled=True), 0, [])  52.3 us
    all_to_all x5, waiting for transfers between devices, copy_for_each(): lax.all_to_all(jnp.broadcast_to(value[None], (devices, *value.shape)), ax...  41.7 us
    all_to_all x5, starting transfers between devices, copy_for_each(): lax.all_to_all(jnp.broadcast_to(value[None], (devices, *value.shape)), ax...  28.7 us
    gather x2, local copies, waits for them, and re-layouts, on_device(): all_owners = jnp.take(doc_ids, all_places)  23 us
  transfers between devices with their start and end apart: 7, of which 6 were waited for; matrix products, arithmetic and copies ran while one was open for 11% of the time, Pallas kernels for 0%

commit v1 on v0

v1 whole, which is shorter than its diff:
```python
import functools

import jax
import jax.numpy as jnp
from jax import lax
from jax.experimental import pallas as pl
from jax.experimental.pallas import tpu as pltpu
from jax.sharding import PartitionSpec as P

HEAD_DIM = 128
SCALE = HEAD_DIM ** (-0.5)
LOG2E = 1.4426950408889634
HIDDEN_SCORE = -2e30
LOWEST = -1e30
CHUNK = 128
DOCS = 4
VMEM_BYTES = 48 * 1024 * 1024
bf16 = jnp.bfloat16
f32 = jnp.float32


def nt(a, b):
    return lax.dot_general(a, b, (((1,), (1,)), ((), ())), preferred_element_type=f32)


def nn(a, b):
    return lax.dot_general(a, b, (((1,), (0,)), ((), ())), preferred_element_type=f32)


def tn(a, b):
    return lax.dot_general(a, b, (((0,), (0,)), ((), ())), preferred_element_type=f32)


def stage(meta, qg, kv, qs, gs, kvs, part):
    sources, rows, width = qg.shape
    half = rows // 2
    grp = width // 2 // HEAD_DIM
    for t in range(2):
        for i in range(sources):
            for g in range(grp):
                at = (i * grp + g) * half
                qs[t, at : at + half, :] = qg[i, t * half : (t + 1) * half, g * HEAD_DIM : (g + 1) * HEAD_DIM]
                gs[t, at : at + half, :] = qg[
                    i, t * half : (t + 1) * half, (grp + g) * HEAD_DIM : (grp + g + 1) * HEAD_DIM
                ]
    for b in range(kv.shape[0] // part):
        to = pl.multiple_of(meta[2 + b] * part, part)
        kvs[pl.ds(to, part), :] = kv[b * part : (b + 1) * part, :]


def block_rows(meta, docs, t, part):
    half = docs.shape[1]
    block = meta[2 + 2 * meta[1] + t]
    own = docs[pl.ds(block, 1), :]
    table = docs[...]
    first = jnp.zeros_like(own)
    for d in range(DOCS - 1):
        ones = (table == d).astype(jnp.int32)
        count = jnp.sum(jnp.sum(ones, axis=0, keepdims=True), axis=1, keepdims=True)
        first = first + jnp.where(own > d, count, 0)
    places = block * half + lax.broadcasted_iota(jnp.int32, (1, half), 1)
    low = (jnp.min(first) // half) * part // CHUNK
    high = (block * part + part - 1) // CHUNK + 1
    return places, first, low, high


def chunk_bias(meta, places, first, c, part, heads):
    half = places.shape[1]
    n = c * CHUNK + lax.broadcasted_iota(jnp.int32, (CHUNK, half), 0)
    keys = (n // part) * half + part * meta[0] + n % part
    seen = (keys <= places) & (keys >= first)
    bias = jnp.where(seen, 0.0, HIDDEN_SCORE)
    return jnp.concatenate([bias] * heads, axis=1)


def forward_kernel(part, meta, docs, qg, kv, stats, qs, gs, kvs):
    stage(meta, qg, kv, qs, gs, kvs, part)
    columns = qs.shape[1]
    heads = columns // docs.shape[1]
    stats[...] = jnp.zeros_like(stats)
    for t in range(2):
        places, first, low, high = block_rows(meta, docs, t, part)

        def body(c, carried, t=t, places=places, first=first):
            peak, total, dot = carried
            at = pl.multiple_of(c * CHUNK, CHUNK)
            k = kvs[pl.ds(at, CHUNK), :HEAD_DIM]
            v = kvs[pl.ds(at, CHUNK), HEAD_DIM:]
            s = nt(k, qs[t]) * (SCALE * LOG2E) + chunk_bias(meta, places, first, c, part, heads)
            dp = nt(v, gs[t])
            new = jnp.maximum(peak, jnp.max(s, axis=0, keepdims=True))
            w = jnp.exp2(s - new)
            factor = jnp.exp2(peak - new)
            total = total * factor + jnp.sum(w, axis=0, keepdims=True)
            dot = dot * factor + jnp.sum(w * dp, axis=0, keepdims=True)
            return new, total, dot

        zero = jnp.zeros((1, columns), f32)
        peak, total, dot = lax.fori_loop(low, high, body, (zero + LOWEST, zero, zero))
        span = slice(t * columns, (t + 1) * columns)
        stats[0:1, span] = peak
        stats[1:2, span] = total
        stats[2:3, span] = dot


def backward_kernel(part, meta, docs, qg, kv, stats, dq, dkv, qs, gs, kvs, acc, dqt):
    stage(meta, qg, kv, qs, gs, kvs, part)
    columns = qs.shape[1]
    half = docs.shape[1]
    heads = columns // half
    sources = stats.shape[0]
    grp = heads // sources
    acc[...] = jnp.zeros_like(acc)
    for t in range(2):
        places, first, low, high = block_rows(meta, docs, t, part)
        span = slice(t * columns, (t + 1) * columns)
        peaks = [stats[i, 0:1, span] for i in range(sources)]
        peak = functools.reduce(jnp.maximum, peaks)
        factors = [jnp.exp2(p - peak) for p in peaks]
        total = sum(stats[i, 1:2, span] * factors[i] for i in range(sources))
        dot = sum(stats[i, 2:3, span] * factors[i] for i in range(sources))
        lse = peak + jnp.log2(total)
        delta = dot / total
        dqt[...] = jnp.zeros_like(dqt)

        def body(c, carried, t=t, places=places, first=first, lse=lse, delta=delta):
            at = pl.multiple_of(c * CHUNK, CHUNK)
            k = kvs[pl.ds(at, CHUNK), :HEAD_DIM]
            v = kvs[pl.ds(at, CHUNK), HEAD_DIM:]
            s = nt(k, qs[t]) * (SCALE * LOG2E) + chunk_bias(meta, places, first, c, part, heads)
            p = jnp.exp2(s - lse)
            dp = nt(v, gs[t])
            ds = (p * (dp - delta)).astype(bf16)
            acc[pl.ds(at, CHUNK), :HEAD_DIM] += nn(ds, qs[t])
            acc[pl.ds(at, CHUNK), HEAD_DIM:] += nn(p.astype(bf16), gs[t])
            dqt[...] += tn(k, ds)
            return carried

        lax.fori_loop(low, high, body, 0)
        for h in range(heads):
            i, g = divmod(h, grp)
            dq[i, t * half : (t + 1) * half, g * HEAD_DIM : (g + 1) * HEAD_DIM] = (
                dqt[:, h * half : (h + 1) * half].T.astype(bf16)
            )
    for b in range(kv.shape[0] // part):
        at = pl.multiple_of(meta[2 + b] * part, part)
        dkv[b * part : (b + 1) * part, :] = acc[pl.ds(at, part), :].astype(bf16)


def home_kernel(parts, low, ab, dkv, payload):
    total = parts[0].astype(f32)
    for o in range(1, parts.shape[0]):
        total = total + parts[o].astype(f32)
    rows = total.shape[0]
    dk = (total[:, :HEAD_DIM] * SCALE).astype(bf16)
    dkv[:, :HEAD_DIM] = dk
    dkv[:, HEAD_DIM:] = total[:, HEAD_DIM:].astype(bf16)
    back = nt(ab[...], dk).astype(bf16)
    low_rank = low[0]
    for o in range(1, low.shape[0]):
        low_rank = low_rank + low[o]
    gb = nn(low_rank.astype(bf16), dk).astype(bf16)
    whole = jnp.concatenate([back, jnp.zeros((back.shape[0], HEAD_DIM - rows), bf16), gb], axis=1)
    for o in range(payload.shape[0]):
        payload[o] = whole


def adapter_kernel(inner_size, meta, parts, hidden, payload):
    heads = parts.shape[0] // inner_size
    rows = hidden.shape[0] // inner_size
    piece = rows // 2
    half = hidden.shape[0] // 2
    ga = None
    gb = None
    for i in range(inner_size):
        back = parts[i].astype(f32)
        for h in range(1, heads):
            back = back + parts[h * inner_size + i].astype(f32)
        mine = jnp.concatenate(
            [hidden[i * piece : (i + 1) * piece, :], hidden[half + i * piece : half + (i + 1) * piece, :]], axis=0
        )
        term = nn(back[:, :rows].astype(bf16), mine)
        ga = term if ga is None else ga + term
        own = parts[meta[0] * inner_size + i].astype(f32)[:, HEAD_DIM:]
        gb = own if gb is None else gb + own
    whole = jnp.concatenate([ga, gb], axis=1).astype(bf16)
    for o in range(payload.shape[0]):
        payload[o] = whole


def final_kernel(parts, ga, gb):
    total = parts[0].astype(f32)
    for o in range(1, parts.shape[0]):
        total = total + parts[o].astype(f32)
    width = ga.shape[0]
    ga[...] = total[:, :width].T
    gb[...] = total[:, width:]


def call(kernel, out_shape, specs, scratch=(), cost=None):
    spaces = {"s": pltpu.SMEM, "v": pltpu.VMEM}
    single = not isinstance(out_shape, tuple)
    return pl.pallas_call(
        kernel,
        out_shape=out_shape,
        in_specs=[pl.BlockSpec(memory_space=spaces[s]) for s in specs],
        out_specs=pl.BlockSpec(memory_space=pltpu.VMEM)
        if single
        else tuple(pl.BlockSpec(memory_space=pltpu.VMEM) for _ in out_shape),
        scratch_shapes=list(scratch),
        compiler_params=pltpu.CompilerParams(vmem_limit_bytes=VMEM_BYTES),
        cost_estimate=cost,
    )


def on_device(queries, keys, values, grad_out, hidden_in, adapter_a, adapter_b, block_order, doc_ids):
    sd = jax.ShapeDtypeStruct
    n_outer, n_inner, n_head = lax.axis_size("outer"), lax.axis_size("inner"), lax.axis_size("head")
    outer, inner, head = lax.axis_index("outer"), lax.axis_index("inner"), lax.axis_index("head")
    tokens = queries.shape[0]
    half = tokens // 2
    part = half // n_inner
    rows = 2 * part
    heads = n_inner * queries.shape[1] // HEAD_DIM
    columns = heads * half
    total_rows = n_outer * rows
    rank = adapter_b.shape[0]

    kv = jnp.concatenate([keys, values], axis=1).reshape(2, n_inner, part, 2 * HEAD_DIM)
    kv = lax.dynamic_index_in_dim(kv, inner, 1, keepdims=False).reshape(rows, 2 * HEAD_DIM)
    qg = jnp.concatenate([queries, grad_out], axis=1)
    qg = lax.all_to_all(jnp.broadcast_to(qg[None], (n_inner, *qg.shape)), "inner", 0, 0, tiled=True)
    kv = lax.all_gather(kv, "outer", axis=0, tiled=True)
    meta = jnp.concatenate([jnp.stack([inner, outer]).astype(jnp.int32), block_order])
    docs = doc_ids.reshape(-1, half)

    low = lax.dot_general(adapter_a, hidden_in, (((0,), (1,)), ((), ())), preferred_element_type=f32)
    low = low.reshape(rank, 2, n_inner, part).transpose(2, 0, 1, 3).reshape(n_inner, rank, rows)
    low = jnp.broadcast_to(low[None], (n_head, n_inner, rank, rows)).reshape(n_head * n_inner, rank, rows)
    low = lax.all_to_all(low, ("head", "inner"), 0, 0, tiled=True)

    staged = [
        pltpu.VMEM((2, columns, HEAD_DIM), bf16),
        pltpu.VMEM((2, columns, HEAD_DIM), bf16),
        pltpu.VMEM((total_rows, 2 * HEAD_DIM), bf16),
    ]
    pair = 2 * columns * total_rows * HEAD_DIM
    stats = call(
        functools.partial(forward_kernel, part),
        sd((4, 2 * columns), f32),
        "svvv",
        staged,
        pl.CostEstimate(flops=2 * pair, bytes_accessed=2 << 20, transcendentals=columns * total_rows),
    )(meta, docs, qg, kv)
    stats = lax.all_gather(stats, "inner", axis=0, tiled=False)
    dq, dkv = call(
        functools.partial(backward_kernel, part),
        (sd((n_inner, tokens, queries.shape[1]), bf16), sd((total_rows, 2 * HEAD_DIM), bf16)),
        "svvvv",
        staged + [pltpu.VMEM((total_rows, 2 * HEAD_DIM), f32), pltpu.VMEM((HEAD_DIM, columns), f32)],
        pl.CostEstimate(flops=5 * pair, bytes_accessed=3 << 20, transcendentals=columns * total_rows),
    )(meta, docs, qg, kv, stats)

    dkv = lax.all_to_all(dkv.reshape(n_outer, rows, 2 * HEAD_DIM), "outer", 0, 0, tiled=True)
    dq = lax.all_to_all(dq, "inner", 0, 0, tiled=True)
    grad_query = (jnp.sum(dq.astype(f32), axis=0) * SCALE).astype(bf16)

    dkv, payload = call(
        home_kernel,
        (sd((rows, 2 * HEAD_DIM), bf16), sd((n_head * n_inner, rank, 2 * HEAD_DIM), bf16)),
        "vvv",
    )(dkv, low, adapter_b)
    payload = lax.all_to_all(payload, ("head", "inner"), 0, 0, tiled=True)
    width = hidden_in.shape[1]
    payload = call(
        functools.partial(adapter_kernel, n_inner), sd((n_outer, rank, width + HEAD_DIM), bf16), "svv"
    )(head.astype(jnp.int32)[None], payload, hidden_in)
    payload = lax.all_to_all(payload, "outer", 0, 0, tiled=True)
    grad_a, grad_b = call(final_kernel, (sd((width, rank), f32), sd((rank, HEAD_DIM), f32)), "v")(payload)

    dkv = lax.all_gather(dkv, "inner", axis=0, tiled=True)
    dkv = dkv.reshape(n_inner, 2, part, 2 * HEAD_DIM).transpose(1, 0, 2, 3).reshape(tokens, 2 * HEAD_DIM)
    return grad_query, dkv[:, :HEAD_DIM], dkv[:, HEAD_DIM:], grad_a, grad_b


def solution(mesh):
    in_specs = (
        P("outer", ("head", "inner")),
        P("outer", "head"),
        P("outer", "head"),
        P("outer", ("head", "inner")),
        P("outer", ("head", "inner")),
        P(("head", "inner"), None),
        P(None, "head"),
        P(),
        P(),
    )
    out_specs = (
        P("outer", ("head", "inner")),
        P("outer", "head"),
        P("outer", "head"),
        P(("head", "inner"), None),
        P(None, "head"),
    )
    return jax.shard_map(on_device, mesh=mesh, in_specs=in_specs, out_specs=out_specs, check_vma=False)
```

time: 278 us -> 161 us (0.58)
  the two profiles are of different devices: /device:TPU:2 before, /device:TPU:64 now
where the time goes in v1:
time: 161 us; the launch traced here: 160 us
  blocking collectives  65.2 us (40%)
  waiting for transfers between devices  43.4 us (27%)
  starting transfers between devices  35.2 us (22%)
  Pallas kernels  8.01 us (5%)
  local copies, waits for them, and re-layouts  4.85 us (3%)
  other arithmetic  2.78 us (2%)
    all_gather x1, blocking collectives, on_device(): kv = lax.all_gather(kv, 'outer', axis=0, tiled=True)  35.4 us
    all_to_all x1, waiting for transfers between devices, on_device(): lax.all_to_all(dkv.reshape(n_outer, rows, 2 * HEAD_DIM), 'outer', 0, 0, t...  26.2 us
    all_to_all x1, blocking collectives, on_device(): payload = lax.all_to_all(payload, ('head', 'inner'), 0, 0, tiled=True)  15.9 us
    all_to_all x1, starting transfers between devices, on_device(): lax.all_to_all(dkv.reshape(n_outer, rows, 2 * HEAD_DIM), 'outer', 0, 0, t...  11.5 us
    all_to_all x1, waiting for transfers between devices, on_device(): dq = lax.all_to_all(dq, 'inner', 0, 0, tiled=True)  9.48 us
    all_to_all x1, starting transfers between devices, on_device(): payload = lax.all_to_all(payload, 'outer', 0, 0, tiled=True)  8.1 us
    all_to_all x1, waiting for transfers between devices, on_device(): payload = lax.all_to_all(payload, 'outer', 0, 0, tiled=True)  7.73 us
    all_to_all x1, starting transfers between devices, on_device(): low = lax.all_to_all(low, ('head', 'inner'), 0, 0, tiled=True)  7.7 us
  transfers between devices with their start and end apart: 5, of which 3 were waited for; matrix products, arithmetic and copies ran while one was open for 3% of the time, Pallas kernels for 4%

profile of v1, /device:TPU:64, one launch (start us, length us, event | category | flops | bytes accessed | tf_op | source)
XLA Modules:
  0.0 160.4 jit_solution(1997078073538172187)
XLA Ops:
  0.6 1.0 pad_maximum_fusion
  1.6 1.1 broadcast_in_dim.16
  2.7 4.4 %all-to-all-start = ((bf16[4,256,512]{2,1,0:T(8,128)(2,1)}), bf16[4,256,512]{2,1,0:T(8,128)(2,1)S(1)}, u32[]{:S(2)}, u32[]{:S(2)}) async-start(bf16[4,256,512]{2,1,0:T(8,128)(2,1)} %broadcast_in_dim.16), calls=%async_computation | async-start | bytes 2097152 | tf_op jit(solution)/shard_map/all_to_all | solution.py:232
  7.6 0.8 reshape.49
  8.5 0.7 copy-done.6
  9.2 35.4 %all_gather.12.kv = bf16[1024,256]{1,0:T(8,128)(2,1)S(1)} all-gather(bf16[64,256]{1,0:T(8,128)(2,1)S(1)} %bitcast.28), channel_id=1, replica_groups=mesh['head'=8,'outer'=16,'inner'=4] {'outer'}, dimensions={0}, use_global_device_ids=true | all-gather | bytes 557056 | tf_op jit(solution)/shard_map/all_gather | solution.py:233
  44.7 7.7 %all-to-all-start.3 = ((f32[32,1,1024]{2,1,0:T(1,128)}), f32[32,1,1024]{2,1,0:T(1,128)S(1)}, u32[]{:S(2)}, u32[]{:S(2)}) async-start(f32[32,1,1024]{2,1,0:T(1,128)} %reshape.49), calls=%async_computation.3 | async-start | bytes 262144 | tf_op jit(solution)/shard_map/all_to_all | solution.py:240
  52.4 2.2 %shard_map.128 = f32[4,2048]{1,0:T(4,128)S(1)} custom-call(s32[34]{0:T(128)S(1)} %pad_add_fusion.meta, s32[32,128]{1,0:T(8,128)S(1)} %bitcast.21, bf16[4,256,512]{2,1,0:T(8,128)(2,1)S(1)} %all-to-all-done.qg, bf16[1024,256]{1,0:T(8,128)(2,1)S(1)} %all_gather.12.kv), custom_call_target="tpu_custom_call" | custom-call | flops 536870912 | bytes 2097152 | tf_op jit(solution)/shard_map/pallas_call | solution.py:248
  54.6 6.9 %all-gather.1.stats = f32[4,4,2048]{2,1,0:T(4,128)S(1)} all-gather(f32[1,4,2048]{2,1,0:T(4,128)S(1)} %bitcast.20), channel_id=2, replica_groups=mesh['head'=8,'outer'=16,'inner'=4] {'inner'}, dimensions={0}, use_global_device_ids=true | all-gather | bytes 163840 | tf_op jit(solution)/shard_map/all_gather | solution.py:255
  61.6 4.1 %shard_map.129 = (bf16[4,256,256]{2,1,0:T(8,128)(2,1)}, bf16[1024,256]{1,0:T(8,128)(2,1)}) custom-call(s32[34]{0:T(128)S(1)} %pad_add_fusion.meta, s32[32,128]{1,0:T(8,128)S(1)} %bitcast.22, bf16[4,256,512]{2,1,0:T(8,128)(2,1)S(1)} %all-to-all-done.qg, bf16[1024,256]{1,0:T(8,128)(2,1)S(1)} %all_gather.12.kv, f32[4,4,2048]{2,1,0:T(4,128)S(1)} %all-gather.1.stats), custom_call_target="tpu_custom_call" | custom-call | flops 1342177280 | bytes 3145728 | tf_op jit(solution)/shard_map/pallas_call | solution.py:256
  65.6 11.5 %all-to-all-start.2 = ((bf16[16,64,256]{2,1,0:T(8,128)(2,1)}), bf16[16,64,256]{2,1,0:T(8,128)(2,1)S(1)}, u32[]{:S(2)}, u32[]{:S(2)}) async-start(bf16[16,64,256]{2,1,0:T(8,128)(2,1)} %bitcast.6), calls=%async_computation.2 | async-start | bytes 1048576 | tf_op jit(solution)/shard_map/all_to_all | solution.py:264
  77.7 0.9 reduce
  78.8 26.2 %all-to-all-done.2.parts = bf16[16,64,256]{2,1,0:T(8,128)(2,1)S(1)} async-done(((bf16[16,64,256]{2,1,0:T(8,128)(2,1)}), bf16[16,64,256]{2,1,0:T(8,128)(2,1)S(1)}, u32[]{:S(2)}, u32[]{:S(2)}) %all-to-all-start.2) | async-done | bytes 524320 | tf_op jit(solution)/shard_map/all_to_all | solution.py:264
  105.2 15.9 %all_to_all.30.parts = bf16[32,16,256]{2,1,0:T(8,128)(2,1)S(1)} all-to-all(bf16[32,16,256]{2,1,0:T(8,128)(2,1)S(1)} %get-tuple-element.14), channel_id=1, replica_groups=mesh['head'=8,'outer'=16,'inner'=4] {'head','inner'}, dimensions={0} | all-to-all | bytes 524288 | tf_op jit(solution)/shard_map/all_to_all | solution.py:273
  121.2 3.5 %all-to-all-start.1 = ((bf16[4,256,256]{2,1,0:T(8,128)(2,1)}), bf16[4,256,256]{2,1,0:T(8,128)(2,1)S(1)}, u32[]{:S(2)}, u32[]{:S(2)}) async-start(bf16[4,256,256]{2,1,0:T(8,128)(2,1)} %get-tuple-element.11), calls=%async_computation.1 | async-start | bytes 1048576 | tf_op jit(solution)/shard_map/all_to_all | solution.py:265
  124.6 0.8 shard_map.131
  125.5 9.5 %all-to-all-done.1 = bf16[4,256,256]{2,1,0:T(8,128)(2,1)S(1)} async-done(((bf16[4,256,256]{2,1,0:T(8,128)(2,1)}), bf16[4,256,256]{2,1,0:T(8,128)(2,1)S(1)}, u32[]{:S(2)}, u32[]{:S(2)}) %all-to-all-start.1) | async-done | bytes 524320 | tf_op jit(solution)/shard_map/all_to_all | solution.py:265
  135.0 8.1 %all-to-all-start.5 = ((bf16[16,16,384]{2,1,0:T(8,128)(2,1)}), bf16[16,16,384]{2,1,0:T(8,128)(2,1)S(1)}, u32[]{:S(2)}, u32[]{:S(2)}) async-start(bf16[16,16,384]{2,1,0:T(8,128)(2,1)} %shard_map.131), calls=%async_computation.5 | async-start | bytes 393216 | tf_op jit(solution)/shard_map/all_to_all | solution.py:278
  143.1 0.7 multiply_convert_fusion
  143.8 6.9 %all_gather.15 = bf16[256,256]{1,0:T(8,128)(2,1)S(1)} all-gather(bf16[64,256]{1,0:T(8,128)(2,1)S(1)} %get-tuple-element.13), channel_id=1, replica_groups=mesh['head'=8,'outer'=16,'inner'=4] {'inner'}, dimensions={0}, use_global_device_ids=true | all-gather | bytes 163840 | tf_op jit(solution)/shard_map/all_gather | solution.py:281
  150.7 0.7 fusion
  151.4 7.7 %all-to-all-done.5.parts = bf16[16,16,384]{2,1,0:T(8,128)(2,1)S(1)} async-done(((bf16[16,16,384]{2,1,0:T(8,128)(2,1)}), bf16[16,16,384]{2,1,0:T(8,128)(2,1)S(1)}, u32[]{:S(2)}, u32[]{:S(2)}) %all-to-all-start.5) | async-done | bytes 196640 | tf_op jit(solution)/shard_map/all_to_all | solution.py:278
  159.1 0.6 shard_map.132
  159.8 0.7 copy.24
  (28 shorter events, 1.5 us)
Async XLA Ops:
  0.6 6.5 %copy-start = (bf16[256,16]{0,1:T(8,128)(2,1)S(1)}, bf16[256,16]{0,1:T(8,128)(2,1)}, u32[]{:S(2)}) copy-start(bf16[256,16]{0,1:T(8,128)(2,1)} %param.14) | copy-start | bytes 24580
  2.7 4.4 %copy-start.1 = (bf16[256,256]{1,0:T(8,128)(2,1)S(1)}, bf16[256,256]{1,0:T(8,128)(2,1)}, u32[]{:S(2)}) copy-start(bf16[256,256]{1,0:T(8,128)(2,1)} %hidden.1) | copy-start | bytes 393220
  2.7 42.0 %all-to-all-start = ((bf16[4,256,512]{2,1,0:T(8,128)(2,1)}), bf16[4,256,512]{2,1,0:T(8,128)(2,1)S(1)}, u32[]{:S(2)}, u32[]{:S(2)}) async-start(bf16[4,256,512]{2,1,0:T(8,128)(2,1)} %broadcast_in_dim.16), calls=%async_computation | async-start | bytes 2097152 | tf_op jit(solution)/shard_map/all_to_all | solution.py:232
  7.6 1.6 copy-start.4
  7.6 1.6 copy-start.5
  8.5 0.7 copy-start.6
  44.7 7.7 %copy-start.3 = (s32[4096]{0:T(1024)S(1)}, s32[4096]{0:T(1024)}, u32[]{:S(2)}) copy-start(s32[4096]{0:T(1024)} %param.17) | copy-start | bytes 49156
  44.7 21.0 %all-to-all-start.3 = ((f32[32,1,1024]{2,1,0:T(1,128)}), f32[32,1,1024]{2,1,0:T(1,128)S(1)}, u32[]{:S(2)}, u32[]{:S(2)}) async-start(f32[32,1,1024]{2,1,0:T(1,128)} %reshape.49), calls=%async_computation.3 | async-start | bytes 262144 | tf_op jit(solution)/shard_map/all_to_all | solution.py:240
  65.6 39.3 %all-to-all-start.2 = ((bf16[16,64,256]{2,1,0:T(8,128)(2,1)}), bf16[16,64,256]{2,1,0:T(8,128)(2,1)S(1)}, u32[]{:S(2)}, u32[]{:S(2)}) async-start(bf16[16,64,256]{2,1,0:T(8,128)(2,1)} %bitcast.6), calls=%async_computation.2 | async-start | bytes 1048576 | tf_op jit(solution)/shard_map/all_to_all | solution.py:264
  78.7 26.3 %copy-start.2 = (bf16[16,128]{1,0:T(8,128)(2,1)S(1)}, bf16[16,128]{1,0:T(8,128)(2,1)}, u32[]{:S(2)}) copy-start(bf16[16,128]{1,0:T(8,128)(2,1)} %ab.1) | copy-start | bytes 12292
  121.2 13.8 %all-to-all-start.1 = ((bf16[4,256,256]{2,1,0:T(8,128)(2,1)}), bf16[4,256,256]{2,1,0:T(8,128)(2,1)S(1)}, u32[]{:S(2)}, u32[]{:S(2)}) async-start(bf16[4,256,256]{2,1,0:T(8,128)(2,1)} %get-tuple-element.11), calls=%async_computation.1 | async-start | bytes 1048576 | tf_op jit(solution)/shard_map/all_to_all | solution.py:265
  135.0 24.2 %all-to-all-start.5 = ((bf16[16,16,384]{2,1,0:T(8,128)(2,1)}), bf16[16,16,384]{2,1,0:T(8,128)(2,1)S(1)}, u32[]{:S(2)}, u32[]{:S(2)}) async-start(bf16[16,16,384]{2,1,0:T(8,128)(2,1)} %shard_map.131), calls=%async_computation.5 | async-start | bytes 393216 | tf_op jit(solution)/shard_map/all_to_all | solution.py:278

commit v2 on v1

v2 whole, which is shorter than its diff:
```python
import functools

import jax
import jax.numpy as jnp
from jax import lax
from jax.experimental import pallas as pl
from jax.experimental.pallas import tpu as pltpu
from jax.sharding import PartitionSpec as P

HEAD_DIM = 128
SCALE = HEAD_DIM ** (-0.5)
LOG2E = 1.4426950408889634
HIDDEN_SCORE = -2e30
LOWEST = -1e30
CHUNK = 128
DOCS = 4
VMEM_BYTES = 48 * 1024 * 1024
bf16 = jnp.bfloat16
f32 = jnp.float32


def nt(a, b):
    return lax.dot_general(a, b, (((1,), (1,)), ((), ())), preferred_element_type=f32)


def nn(a, b):
    return lax.dot_general(a, b, (((1,), (0,)), ((), ())), preferred_element_type=f32)


def tn(a, b):
    return lax.dot_general(a, b, (((0,), (0,)), ((), ())), preferred_element_type=f32)


def stage(order, q, g, kv, qs, gs, kvs, part):
    sources, tokens, width = q.shape
    half = tokens // 2
    grp = width // HEAD_DIM
    for t in range(2):
        for i in range(sources):
            for n in range(grp):
                at = (i * grp + n) * half
                span = slice(n * HEAD_DIM, (n + 1) * HEAD_DIM)
                qs[t, at : at + half, :] = q[i, t * half : (t + 1) * half, span]
                gs[t, at : at + half, :] = g[i, t * half : (t + 1) * half, span]
    for b in range(kv.shape[0] // part):
        to = pl.multiple_of(order[b] * part, part)
        kvs[pl.ds(to, part), :] = kv[b * part : (b + 1) * part, :]


def block_rows(order, outer, docs, t, part):
    half = docs.shape[1]
    block = order[2 * outer[0] + t]
    own = docs[pl.ds(block, 1), :]
    table = docs[...]
    first = jnp.zeros_like(own)
    for d in range(DOCS - 1):
        ones = (table == d).astype(jnp.int32)
        count = jnp.sum(jnp.sum(ones, axis=0, keepdims=True), axis=1, keepdims=True)
        first = first + jnp.where(own > d, count, 0)
    places = block * half + lax.broadcasted_iota(jnp.int32, (1, half), 1)
    low = (jnp.min(first) // half) * part // CHUNK
    high = (block * part + part - 1) // CHUNK + 1
    return places, first, low, high


def chunk_bias(inner, places, first, c, part, heads):
    half = places.shape[1]
    n = c * CHUNK + lax.broadcasted_iota(jnp.int32, (CHUNK, half), 0)
    keys = (n // part) * half + part * inner[0] + n % part
    seen = (keys <= places) & (keys >= first)
    bias = jnp.where(seen, 0.0, HIDDEN_SCORE)
    return jnp.concatenate([bias] * heads, axis=1)


def forward_kernel(part, inner, outer, order, docs, q, g, kv, lows, stats, low, qs, gs, kvs):
    stage(order, q, g, kv, qs, gs, kvs, part)
    columns = qs.shape[1]
    heads = columns // docs.shape[1]
    stats[...] = jnp.zeros_like(stats)
    whole = lows[0].astype(f32)
    for i in range(1, lows.shape[0]):
        whole = whole + lows[i].astype(f32)
    half = docs.shape[1]
    shift = (half - part * inner[0]) % half
    mine = [pltpu.roll(whole[:, t * half : (t + 1) * half], shift, 1)[:, :part] for t in range(2)]
    low[...] = jnp.concatenate(mine, axis=1)
    for t in range(2):
        places, first, low_chunk, high = block_rows(order, outer, docs, t, part)

        def body(c, carried, t=t, places=places, first=first):
            peak, total, dot = carried
            at = pl.multiple_of(c * CHUNK, CHUNK)
            k = kvs[pl.ds(at, CHUNK), :HEAD_DIM]
            v = kvs[pl.ds(at, CHUNK), HEAD_DIM:]
            s = nt(k, qs[t]) * (SCALE * LOG2E) + chunk_bias(inner, places, first, c, part, heads)
            dp = nt(v, gs[t])
            new = jnp.maximum(peak, jnp.max(s, axis=0, keepdims=True))
            w = jnp.exp2(s - new)
            factor = jnp.exp2(peak - new)
            total = total * factor + jnp.sum(w, axis=0, keepdims=True)
            dot = dot * factor + jnp.sum(w * dp, axis=0, keepdims=True)
            return new, total, dot

        zero = jnp.zeros((1, columns), f32)
        peak, total, dot = lax.fori_loop(low_chunk, high, body, (zero + LOWEST, zero, zero))
        span = slice(t * columns, (t + 1) * columns)
        stats[0:1, span] = peak
        stats[1:2, span] = total
        stats[2:3, span] = dot


def row_terms(stats, t, columns):
    sources = stats.shape[0]
    span = slice(t * columns, (t + 1) * columns)
    peaks = [stats[i, 0:1, span] for i in range(sources)]
    peak = functools.reduce(jnp.maximum, peaks)
    factors = [jnp.exp2(p - peak) for p in peaks]
    total = sum(stats[i, 1:2, span] * factors[i] for i in range(sources))
    dot = sum(stats[i, 2:3, span] * factors[i] for i in range(sources))
    return peak + jnp.log2(total), dot / total


def key_kernel(part, inner, outer, order, docs, q, g, kv, stats, dkv, qs, gs, kvs, acc):
    stage(order, q, g, kv, qs, gs, kvs, part)
    columns = qs.shape[1]
    heads = columns // docs.shape[1]
    acc[...] = jnp.zeros_like(acc)
    for t in range(2):
        places, first, low_chunk, high = block_rows(order, outer, docs, t, part)
        lse, delta = row_terms(stats, t, columns)

        def body(c, carried, t=t, places=places, first=first, lse=lse, delta=delta):
            at = pl.multiple_of(c * CHUNK, CHUNK)
            k = kvs[pl.ds(at, CHUNK), :HEAD_DIM]
            v = kvs[pl.ds(at, CHUNK), HEAD_DIM:]
            s = nt(k, qs[t]) * (SCALE * LOG2E) + chunk_bias(inner, places, first, c, part, heads)
            p = jnp.exp2(s - lse)
            ds = (p * (nt(v, gs[t]) - delta)).astype(bf16)
            acc[pl.ds(at, CHUNK), :HEAD_DIM] += nn(ds, qs[t])
            acc[pl.ds(at, CHUNK), HEAD_DIM:] += nn(p.astype(bf16), gs[t])
            return carried

        lax.fori_loop(low_chunk, high, body, 0)
    for z in range(dkv.shape[0]):
        for t in range(2):
            at = pl.multiple_of(order[2 * z + t] * part, part)
            dkv[z, t * part : (t + 1) * part, :] = acc[pl.ds(at, part), :].astype(bf16)


def query_kernel(part, inner, outer, order, docs, q, g, kv, stats, dq, qs, gs, kvs, dqt):
    stage(order, q, g, kv, qs, gs, kvs, part)
    columns = qs.shape[1]
    half = docs.shape[1]
    heads = columns // half
    grp = heads // stats.shape[0]
    for t in range(2):
        places, first, low_chunk, high = block_rows(order, outer, docs, t, part)
        lse, delta = row_terms(stats, t, columns)
        dqt[...] = jnp.zeros_like(dqt)

        def body(c, carried, t=t, places=places, first=first, lse=lse, delta=delta):
            at = pl.multiple_of(c * CHUNK, CHUNK)
            k = kvs[pl.ds(at, CHUNK), :HEAD_DIM]
            v = kvs[pl.ds(at, CHUNK), HEAD_DIM:]
            s = nt(k, qs[t]) * (SCALE * LOG2E) + chunk_bias(inner, places, first, c, part, heads)
            dqt[...] += tn(k, (jnp.exp2(s - lse) * (nt(v, gs[t]) - delta)).astype(bf16))
            return carried

        lax.fori_loop(low_chunk, high, body, 0)
        for h in range(heads):
            i, n = divmod(h, grp)
            dq[i, t * half : (t + 1) * half, n * HEAD_DIM : (n + 1) * HEAD_DIM] = (
                dqt[:, h * half : (h + 1) * half].T.astype(bf16)
            )


def spread_kernel(part, inner, keys, values, kv, held, arrived):
    half = keys.shape[0] // 2
    copies = []
    for t in range(2):
        here = pl.multiple_of(t * half + inner[0] * part, part)
        for n, source in enumerate((keys, values)):
            copy = pltpu.make_async_copy(
                source.at[pl.ds(here, part), :],
                held.at[t * part : (t + 1) * part, n * HEAD_DIM : (n + 1) * HEAD_DIM],
                arrived.at[2 * t + n],
            )
            copy.start()
            copies.append(copy)
    for copy in copies:
        copy.wait()
    whole = held[...]
    for o in range(kv.shape[0]):
        kv[o] = whole


def home_kernel(parts, ab, low, dkv, payload):
    total = parts[0].astype(f32)
    for o in range(1, parts.shape[0]):
        total = total + parts[o].astype(f32)
    dk = (total[:, :HEAD_DIM] * SCALE).astype(bf16)
    dkv[:, :HEAD_DIM] = dk
    dkv[:, HEAD_DIM:] = total[:, HEAD_DIM:].astype(bf16)
    back = nt(ab[...], dk)
    rank, rows = back.shape
    whole = jnp.concatenate([back, low[...]], axis=1).astype(bf16)
    for o in range(payload.shape[0]):
        payload[o] = whole


def adapter_kernel(inner_size, parts, dkv, hidden, payload):
    heads = parts.shape[0] // inner_size
    rows = hidden.shape[0] // inner_size
    piece = rows // 2
    half = hidden.shape[0] // 2
    ga = None
    gb = None
    for i in range(inner_size):
        both = parts[i].astype(f32)
        for h in range(1, heads):
            both = both + parts[h * inner_size + i].astype(f32)
        both = both.astype(bf16)
        here, there = i * piece, half + i * piece
        mine = jnp.concatenate([hidden[here : here + piece, :], hidden[there : there + piece, :]], axis=0)
        term = nn(both[:, :rows], mine)
        ga = term if ga is None else ga + term
        term = nn(both[:, rows:], dkv[i * rows : (i + 1) * rows, :HEAD_DIM])
        gb = term if gb is None else gb + term
    whole = jnp.concatenate([ga, gb], axis=1).astype(bf16)
    for o in range(payload.shape[0]):
        payload[o] = whole


def final_kernel(parts, ga, gb):
    total = parts[0].astype(f32)
    for o in range(1, parts.shape[0]):
        total = total + parts[o].astype(f32)
    width = ga.shape[1]
    ga[...] = total[:, :width]
    gb[...] = total[:, width:]


def call(kernel, out_shape, specs, scratch=(), cost=None, vmem=VMEM_BYTES):
    spaces = {"s": pltpu.SMEM, "v": pltpu.VMEM, "h": pltpu.HBM}
    single = not isinstance(out_shape, tuple)
    return pl.pallas_call(
        kernel,
        out_shape=out_shape,
        in_specs=[pl.BlockSpec(memory_space=spaces[s]) for s in specs],
        out_specs=pl.BlockSpec(memory_space=pltpu.VMEM)
        if single
        else tuple(pl.BlockSpec(memory_space=pltpu.VMEM) for _ in out_shape),
        scratch_shapes=list(scratch),
        compiler_params=pltpu.CompilerParams(vmem_limit_bytes=vmem),
        cost_estimate=cost,
    )


def on_device(queries, keys, values, grad_out, hidden_in, adapter_a, adapter_b, block_order, doc_ids):
    sd = jax.ShapeDtypeStruct
    n_outer, n_inner, n_head = lax.axis_size("outer"), lax.axis_size("inner"), lax.axis_size("head")
    outer, inner = lax.axis_index("outer"), lax.axis_index("inner")
    tokens = queries.shape[0]
    half = tokens // 2
    part = half // n_inner
    rows = 2 * part
    heads = n_inner * queries.shape[1] // HEAD_DIM
    columns = heads * half
    total_rows = n_outer * rows
    rank = adapter_b.shape[0]

    width = hidden_in.shape[1]
    ids = (inner.astype(jnp.int32)[None], outer.astype(jnp.int32)[None])
    docs = doc_ids.reshape(-1, half)
    kv = call(
        functools.partial(spread_kernel, part),
        sd((n_outer, rows, 2 * HEAD_DIM), bf16),
        "shh",
        [pltpu.VMEM((rows, 2 * HEAD_DIM), bf16), pltpu.SemaphoreType.DMA((4,))],
        vmem=None,
    )(ids[0], keys, values)
    kv = lax.all_to_all(kv, "outer", 0, 0, tiled=True)
    q = lax.all_gather(queries, "inner", axis=0, tiled=False)
    g = lax.all_gather(grad_out, "inner", axis=0, tiled=False)
    lows = lax.all_gather(nt(adapter_a.T, hidden_in).astype(bf16), "inner", axis=0, tiled=False)
    kv, q, g, lows = lax.optimization_barrier((kv, q, g, lows))
    kv = kv.reshape(total_rows, 2 * HEAD_DIM)

    staged = [
        pltpu.VMEM((2, columns, HEAD_DIM), bf16),
        pltpu.VMEM((2, columns, HEAD_DIM), bf16),
        pltpu.VMEM((total_rows, 2 * HEAD_DIM), bf16),
    ]
    pair = 2 * columns * total_rows * HEAD_DIM
    stats, low = call(
        functools.partial(forward_kernel, part),
        (sd((4, 2 * columns), f32), sd((rank, rows), f32)),
        "sssvvvvv",
        staged,
        pl.CostEstimate(flops=2 * pair, bytes_accessed=2 << 20, transcendentals=columns * total_rows),
    )(*ids, block_order, docs, q, g, kv, lows)
    stats = lax.all_gather(stats, "inner", axis=0, tiled=False)
    dkv = call(
        functools.partial(key_kernel, part),
        sd((n_outer, rows, 2 * HEAD_DIM), bf16),
        "sssvvvvv",
        staged + [pltpu.VMEM((total_rows, 2 * HEAD_DIM), f32)],
        pl.CostEstimate(flops=4 * pair, bytes_accessed=3 << 20, transcendentals=columns * total_rows),
    )(*ids, block_order, docs, q, g, kv, stats)
    dkv, stats = lax.optimization_barrier((dkv, stats))
    dq = call(
        functools.partial(query_kernel, part),
        sd((n_inner, tokens, queries.shape[1]), bf16),
        "sssvvvvv",
        staged + [pltpu.VMEM((HEAD_DIM, columns), f32)],
        pl.CostEstimate(flops=3 * pair, bytes_accessed=3 << 20, transcendentals=columns * total_rows),
    )(*ids, block_order, docs, q, g, kv, stats)

    home = lax.all_to_all(dkv, "outer", 0, 0, tiled=True)
    own = lax.dynamic_index_in_dim(dq, inner, 0, keepdims=False).astype(f32)
    for d in range(1, n_inner):
        sent = lax.dynamic_index_in_dim(dq, inner ^ d, 0, keepdims=False)
        own = own + lax.ppermute(sent, "inner", [(i, i ^ d) for i in range(n_inner)]).astype(f32)
    grad_query = (own * SCALE).astype(bf16)

    home, grad_query = lax.optimization_barrier((home, grad_query))
    dkv, payload = call(
        home_kernel,
        (sd((rows, 2 * HEAD_DIM), bf16), sd((n_head * n_inner, rank, 2 * rows), bf16)),
        "vvv",
    )(home, adapter_b, low)
    payload = lax.all_to_all(payload, ("head", "inner"), 0, 0, tiled=True)
    dkv = lax.all_gather(dkv, "inner", axis=0, tiled=True)
    payload = call(
        functools.partial(adapter_kernel, n_inner), sd((n_outer, rank, width + HEAD_DIM), bf16), "vvv"
    )(payload, dkv, hidden_in)
    payload = lax.all_to_all(payload, "outer", 0, 0, tiled=True)

    dkv = dkv.reshape(n_inner, 2, part, 2 * HEAD_DIM).transpose(1, 0, 2, 3).reshape(tokens, 2 * HEAD_DIM)
    grad_key, grad_value = dkv[:, :HEAD_DIM], dkv[:, HEAD_DIM:]
    payload, grad_query, grad_key, grad_value = lax.optimization_barrier(
        (payload, grad_query, grad_key, grad_value)
    )
    grad_a, grad_b = call(final_kernel, (sd((rank, width), f32), sd((rank, HEAD_DIM), f32)), "v")(payload)
    return grad_query, grad_key, grad_value, grad_a.T, grad_b


def solution(mesh):
    in_specs = (
        P("outer", ("head", "inner")),
        P("outer", "head"),
        P("outer", "head"),
        P("outer", ("head", "inner")),
        P("outer", ("head", "inner")),
        P(("head", "inner"), None),
        P(None, "head"),
        P(),
        P(),
    )
    out_specs = (
        P("outer", ("head", "inner")),
        P("outer", "head"),
        P("outer", "head"),
        P(("head", "inner"), None),
        P(None, "head"),
    )
    return jax.shard_map(on_device, mesh=mesh, in_specs=in_specs, out_specs=out_specs, check_vma=False)
```

time: 161 us -> 141 us (0.88)
  the two profiles are of different devices: /device:TPU:64 before, /device:TPU:32 now
where the time goes in v2:
time: 141 us; the launch traced here: 140 us
  starting transfers between devices  49 us (35%)
  blocking collectives  38.8 us (28%)
  waiting for transfers between devices  36.8 us (26%)
  Pallas kernels  12.6 us (9%)
    all_to_all x1, waiting for transfers between devices, on_device(): payload = lax.all_to_all(payload, 'outer', 0, 0, tiled=True)  15.9 us
    all_to_all x1, starting transfers between devices, on_device(): kv = lax.all_to_all(kv, 'outer', 0, 0, tiled=True)  15.4 us
    all_to_all x1, starting transfers between devices, on_device(): home = lax.all_to_all(dkv, 'outer', 0, 0, tiled=True)  11.2 us
    all_to_all x1, waiting for transfers between devices, on_device(): home = lax.all_to_all(dkv, 'outer', 0, 0, tiled=True)  10.6 us
    ppermute x3, starting transfers between devices, on_device(): lax.ppermute(sent, 'inner', [(i, i ^ d) for i in range(n_inner)])  9.09 us
    all_gather x1, blocking collectives, on_device(): g = lax.all_gather(grad_out, 'inner', axis=0, tiled=False)  8.91 us
    all_gather x1, blocking collectives, on_device(): q = lax.all_gather(queries, 'inner', axis=0, tiled=False)  8.89 us
    all_gather x1, blocking collectives, on_device(): dkv = lax.all_gather(dkv, 'inner', axis=0, tiled=True)  7.32 us
  transfers between devices with their start and end apart: 7, of which 6 were waited for; matrix products, arithmetic and copies ran while one was open for 1% of the time, Pallas kernels for 2%

profile of v2, /device:TPU:32, one launch (start us, length us, event | category | flops | bytes accessed | tf_op | source)
XLA Modules:
  0.0 140.2 jit_solution(5969814823651291404)
XLA Ops:
  0.7 1.6 %shard_map.128 = bf16[16,64,256]{2,1,0:T(8,128)(2,1)} custom-call(s32[1]{0:T(128)} %bitcast.inner, bf16[256,128]{1,0:T(8,128)(2,1)} %keys.1, bf16[256,128]{1,0:T(8,128)(2,1)} %values.1), custom_call_target="tpu_custom_call" | custom-call | tf_op jit(solution)/shard_map/pallas_call | solution.py:275
  2.3 15.4 %all-to-all-start = ((bf16[16,64,256]{2,1,0:T(8,128)(2,1)}), bf16[16,64,256]{2,1,0:T(8,128)(2,1)S(1)}, u32[]{:S(2)}, u32[]{:S(2)}) async-start(bf16[16,64,256]{2,1,0:T(8,128)(2,1)} %shard_map.128), calls=%async_computation | async-start | bytes 1048576 | tf_op jit(solution)/shard_map/all_to_all | solution.py:282
  17.8 6.7 %all-gather.2 = bf16[64,256]{1,0:T(8,128)(2,1)S(1)} all-gather(bf16[16,256]{1,0:T(8,128)(2,1)S(1)} %convolution_convert_fusion), channel_id=4, replica_groups=mesh['head'=8,'outer'=16,'inner'=4] {'inner'}, dimensions={0}, use_global_device_ids=true | all-gather | bytes 40960 | tf_op jit(solution)/shard_map/all_gather | solution.py:285
  24.6 8.9 %all-gather = bf16[1024,256]{1,0:T(8,128)(2,1)S(1)} all-gather(bf16[256,256]{1,0:T(8,128)(2,1)S(1)} %copy-done.5), channel_id=2, replica_groups=mesh['head'=8,'outer'=16,'inner'=4] {'inner'}, dimensions={0}, use_global_device_ids=true | all-gather | bytes 655360 | tf_op jit(solution)/shard_map/all_gather | solution.py:283
  33.5 8.9 %all-gather.1 = bf16[1024,256]{1,0:T(8,128)(2,1)S(1)} all-gather(bf16[256,256]{1,0:T(8,128)(2,1)S(1)} %copy-done.6), channel_id=3, replica_groups=mesh['head'=8,'outer'=16,'inner'=4] {'inner'}, dimensions={0}, use_global_device_ids=true | all-gather | bytes 655360 | tf_op jit(solution)/shard_map/all_gather | solution.py:284
  42.4 3.5 %all-to-all-done = bf16[16,64,256]{2,1,0:T(8,128)(2,1)S(1)} async-done(((bf16[16,64,256]{2,1,0:T(8,128)(2,1)}), bf16[16,64,256]{2,1,0:T(8,128)(2,1)S(1)}, u32[]{:S(2)}, u32[]{:S(2)}) %all-to-all-start) | async-done | bytes 524320 | tf_op jit(solution)/shard_map/all_to_all | solution.py:282
  46.6 2.2 %shard_map.129 = (f32[4,2048]{1,0:T(4,128)S(1)}, f32[16,64]{1,0:T(8,128)S(1)}) custom-call(s32[1]{0:T(128)} %bitcast.inner, s32[1]{0:T(128)} %bitcast.1.outer, s32[32]{0:T(128)S(1)} %copy-done.4, s32[32,128]{1,0:T(8,128)S(1)} %bitcast.36, bf16[4,256,256]{2,1,0:T(8,128)(2,1)S(1)} %bitcast.25, bf16[4,256,256]{2,1,0:T(8,128)(2,1)S(1)} %bitcast.28, ...), custom_call_target="tpu_custom_call" | custom-call | flops 536870912 | bytes 2097152 | tf_op jit(solution)/shard_map/pallas_call | solution.py:295
  48.8 6.9 %all-gather.4.stats = f32[4,4,2048]{2,1,0:T(4,128)S(1)} all-gather(f32[1,4,2048]{2,1,0:T(4,128)S(1)} %bitcast.34), channel_id=5, replica_groups=mesh['head'=8,'outer'=16,'inner'=4] {'inner'}, dimensions={0}, use_global_device_ids=true | all-gather | bytes 163840 | tf_op jit(solution)/shard_map/all_gather | solution.py:302
  55.7 3.6 %shard_map.130 = bf16[16,64,256]{2,1,0:T(8,128)(2,1)} custom-call(s32[1]{0:T(128)} %bitcast.inner, s32[1]{0:T(128)} %bitcast.1.outer, s32[32]{0:T(128)S(1)} %copy-done.4, s32[32,128]{1,0:T(8,128)S(1)} %bitcast.37, bf16[4,256,256]{2,1,0:T(8,128)(2,1)S(1)} %bitcast.26, bf16[4,256,256]{2,1,0:T(8,128)(2,1)S(1)} %bitcast.29, bf16[1024,256]{1,0:T(8,128)(2,1)S(1)} %bitcast.32, ...), custom_call_target="tpu_custom_call" | custom-call | flops 1073741824 | bytes 3145728 | tf_op jit(solution)/shard_map/pallas_call | solution.py:303
  59.3 11.2 %all-to-all-start.1 = ((bf16[16,64,256]{2,1,0:T(8,128)(2,1)}), bf16[16,64,256]{2,1,0:T(8,128)(2,1)S(1)}, u32[]{:S(2)}, u32[]{:S(2)}) async-start(bf16[16,64,256]{2,1,0:T(8,128)(2,1)} %shard_map.130), calls=%async_computation.1 | async-start | bytes 1048576 | tf_op jit(solution)/shard_map/all_to_all | solution.py:319
  70.5 2.7 %shard_map.131 = bf16[4,256,256]{2,1,0:T(8,128)(2,1)S(1)} custom-call(s32[1]{0:T(128)} %bitcast.inner, s32[1]{0:T(128)} %bitcast.1.outer, s32[32]{0:T(128)S(1)} %copy-done.4, s32[32,128]{1,0:T(8,128)S(1)} %bitcast.38, bf16[4,256,256]{2,1,0:T(8,128)(2,1)S(1)} %bitcast.27, bf16[4,256,256]{2,1,0:T(8,128)(2,1)S(1)} %bitcast.30, bf16[1024,256]{1,0:T(8,128)(2,1)S(1)} %bitcast.33, ...), custom_call_target="tpu_custom_call" | custom-call | flops 805306368 | bytes 3145728 | tf_op jit(solution)/shard_map/pallas_call | solution.py:311
  73.3 1.9 %collective-permute-start = (bf16[256,256]{1,0:T(8,128)(2,1)S(1)}, bf16[256,256]{1,0:T(8,128)(2,1)S(1)}, u32[]{:S(2)}, u32[]{:S(2)}) collective-permute-start(bf16[256,256]{1,0:T(8,128)(2,1)S(1)} %get-tuple-element.41), channel_id=1, source_target_pairs={{0,1},{1,0},{2,3},{3,2},{4,5},{5,4},{6,7},{7,6},{8,9},{9,8},{10,11... | collective-permute-start | bytes 393224 | tf_op jit(solution)/shard_map/ppermute | solution.py:323
  75.2 4.9 %collective-permute-start.1 = (bf16[256,256]{1,0:T(8,128)(2,1)S(1)}, bf16[256,256]{1,0:T(8,128)(2,1)S(1)}, u32[]{:S(2)}, u32[]{:S(2)}) collective-permute-start(bf16[256,256]{1,0:T(8,128)(2,1)S(1)} %get-tuple-element.43), channel_id=1, source_target_pairs={{0,2},{1,3},{2,0},{3,1},{4,6},{5,7},{6,4},{7,5},{8,10},{9,11},{10,... | collective-permute-start | bytes 393224 | tf_op jit(solution)/shard_map/ppermute | solution.py:323
  80.1 2.3 %collective-permute-start.2 = (bf16[256,256]{1,0:T(8,128)(2,1)S(1)}, bf16[256,256]{1,0:T(8,128)(2,1)S(1)}, u32[]{:S(2)}, u32[]{:S(2)}) collective-permute-start(bf16[256,256]{1,0:T(8,128)(2,1)S(1)} %get-tuple-element.42), channel_id=1, source_target_pairs={{0,3},{1,2},{2,1},{3,0},{4,7},{5,6},{6,5},{7,4},{8,11},{9,10},{10,... | collective-permute-start | bytes 393224 | tf_op jit(solution)/shard_map/ppermute | solution.py:323
  82.4 2.1 %collective-permute-done.1 = bf16[256,256]{1,0:T(8,128)(2,1)S(1)} collective-permute-done((bf16[256,256]{1,0:T(8,128)(2,1)S(1)}, bf16[256,256]{1,0:T(8,128)(2,1)S(1)}, u32[]{:S(2)}, u32[]{:S(2)}) %collective-permute-start.1) | collective-permute-done | bytes 131104 | tf_op jit(solution)/shard_map/ppermute | solution.py:323
  84.5 4.5 %collective-permute-done.2 = bf16[256,256]{1,0:T(8,128)(2,1)S(1)} collective-permute-done((bf16[256,256]{1,0:T(8,128)(2,1)S(1)}, bf16[256,256]{1,0:T(8,128)(2,1)S(1)}, u32[]{:S(2)}, u32[]{:S(2)}) %collective-permute-start.2) | collective-permute-done | bytes 131104 | tf_op jit(solution)/shard_map/ppermute | solution.py:323
  89.0 0.7 fusion.3
  89.7 10.6 %all-to-all-done.1.parts = bf16[16,64,256]{2,1,0:T(8,128)(2,1)S(1)} async-done(((bf16[16,64,256]{2,1,0:T(8,128)(2,1)}), bf16[16,64,256]{2,1,0:T(8,128)(2,1)S(1)}, u32[]{:S(2)}, u32[]{:S(2)}) %all-to-all-start.1) | async-done | bytes 524320 | tf_op jit(solution)/shard_map/all_to_all | solution.py:319
  100.3 0.8 shard_map.132
  101.1 7.3 %all-to-all-start.2 = ((bf16[32,16,128]{2,1,0:T(8,128)(2,1)}), bf16[32,16,128]{2,1,0:T(8,128)(2,1)S(1)}, u32[]{:S(2)}, u32[]{:S(2)}) async-start(bf16[32,16,128]{2,1,0:T(8,128)(2,1)} %get-tuple-element.32), calls=%async_computation.2 | async-start | bytes 262144 | tf_op jit(solution)/shard_map/all_to_all | solution.py:332
  108.5 7.3 %all_gather.35.dkv = bf16[256,256]{1,0:T(8,128)(2,1)S(1)} all-gather(bf16[64,256]{1,0:T(8,128)(2,1)S(1)} %get-tuple-element.33), channel_id=1, replica_groups=mesh['head'=8,'outer'=16,'inner'=4] {'inner'}, dimensions={0}, use_global_device_ids=true | all-gather | bytes 163840 | tf_op jit(solution)/shard_map/all_gather | solution.py:333
  116.0 0.9 shard_map.133
  116.9 6.1 %all-to-all-start.3 = ((bf16[16,16,384]{2,1,0:T(8,128)(2,1)}), bf16[16,16,384]{2,1,0:T(8,128)(2,1)S(1)}, u32[]{:S(2)}, u32[]{:S(2)}) async-start(bf16[16,16,384]{2,1,0:T(8,128)(2,1)} %shard_map.133), calls=%async_computation.3 | async-start | bytes 393216 | tf_op jit(solution)/shard_map/all_to_all | solution.py:337
  123.7 15.9 %all-to-all-done.3.parts = bf16[16,16,384]{2,1,0:T(8,128)(2,1)S(1)} async-done(((bf16[16,16,384]{2,1,0:T(8,128)(2,1)}), bf16[16,16,384]{2,1,0:T(8,128)(2,1)S(1)}, u32[]{:S(2)}, u32[]{:S(2)}) %all-to-all-start.3) | async-done | bytes 196640 | tf_op jit(solution)/shard_map/all_to_all | solution.py:337
  (21 shorter events, 2.4 us)
Async XLA Ops:
  0.6 17.0 %copy-start = (bf16[256,16]{0,1:T(8,128)(2,1)S(1)}, bf16[256,16]{0,1:T(8,128)(2,1)}, u32[]{:S(2)}) copy-start(bf16[256,16]{0,1:T(8,128)(2,1)} %param.14) | copy-start | bytes 24580
  2.3 15.4 %copy-start.1 = (bf16[256,256]{1,0:T(8,128)(2,1)S(1)}, bf16[256,256]{1,0:T(8,128)(2,1)}, u32[]{:S(2)}) copy-start(bf16[256,256]{1,0:T(8,128)(2,1)} %hidden.1) | copy-start | bytes 393220
  2.3 43.6 %all-to-all-start = ((bf16[16,64,256]{2,1,0:T(8,128)(2,1)}), bf16[16,64,256]{2,1,0:T(8,128)(2,1)S(1)}, u32[]{:S(2)}, u32[]{:S(2)}) async-start(bf16[16,64,256]{2,1,0:T(8,128)(2,1)} %shard_map.128), calls=%async_computation | async-start | bytes 1048576 | tf_op jit(solution)/shard_map/all_to_all | solution.py:282
  17.7 6.9 %copy-start.5 = (bf16[256,256]{1,0:T(8,128)(2,1)S(1)}, bf16[256,256]{1,0:T(8,128)(2,1)}, u32[]{:S(2)}) copy-start(bf16[256,256]{1,0:T(8,128)(2,1)} %param.9) | copy-start | bytes 393220
  24.6 8.9 %copy-start.6 = (bf16[256,256]{1,0:T(8,128)(2,1)S(1)}, bf16[256,256]{1,0:T(8,128)(2,1)}, u32[]{:S(2)}) copy-start(bf16[256,256]{1,0:T(8,128)(2,1)} %param.12) | copy-start | bytes 393220
  33.5 12.4 %copy-start.3 = (s32[4096]{0:T(1024)S(1)}, s32[4096]{0:T(1024)}, u32[]{:S(2)}) copy-start(s32[4096]{0:T(1024)} %param.17) | copy-start | bytes 49156
  45.9 0.7 copy-start.4
  59.3 40.9 %all-to-all-start.1 = ((bf16[16,64,256]{2,1,0:T(8,128)(2,1)}), bf16[16,64,256]{2,1,0:T(8,128)(2,1)S(1)}, u32[]{:S(2)}, u32[]{:S(2)}) async-start(bf16[16,64,256]{2,1,0:T(8,128)(2,1)} %shard_map.130), calls=%async_computation.1 | async-start | bytes 1048576 | tf_op jit(solution)/shard_map/all_to_all | solution.py:319
  73.3 9.1 %collective-permute-start = (bf16[256,256]{1,0:T(8,128)(2,1)S(1)}, bf16[256,256]{1,0:T(8,128)(2,1)S(1)}, u32[]{:S(2)}, u32[]{:S(2)}) collective-permute-start(bf16[256,256]{1,0:T(8,128)(2,1)S(1)} %get-tuple-element.41), channel_id=1, source_target_pairs={{0,1},{1,0},{2,3},{3,2},{4,5},{5,4},{6,7},{7,6},{8,9},{9,8},{10,11... | collective-permute-start | bytes 393224 | tf_op jit(solution)/shard_map/ppermute | solution.py:323
  75.2 9.3 %collective-permute-start.1 = (bf16[256,256]{1,0:T(8,128)(2,1)S(1)}, bf16[256,256]{1,0:T(8,128)(2,1)S(1)}, u32[]{:S(2)}, u32[]{:S(2)}) collective-permute-start(bf16[256,256]{1,0:T(8,128)(2,1)S(1)} %get-tuple-element.43), channel_id=1, source_target_pairs={{0,2},{1,3},{2,0},{3,1},{4,6},{5,7},{6,4},{7,5},{8,10},{9,11},{10,... | collective-permute-start | bytes 393224 | tf_op jit(solution)/shard_map/ppermute | solution.py:323
  80.1 8.9 %collective-permute-start.2 = (bf16[256,256]{1,0:T(8,128)(2,1)S(1)}, bf16[256,256]{1,0:T(8,128)(2,1)S(1)}, u32[]{:S(2)}, u32[]{:S(2)}) collective-permute-start(bf16[256,256]{1,0:T(8,128)(2,1)S(1)} %get-tuple-element.42), channel_id=1, source_target_pairs={{0,3},{1,2},{2,1},{3,0},{4,7},{5,6},{6,5},{7,4},{8,11},{9,10},{10,... | collective-permute-start | bytes 393224 | tf_op jit(solution)/shard_map/ppermute | solution.py:323
  89.0 11.3 %copy-start.2 = (bf16[16,128]{1,0:T(8,128)(2,1)S(1)}, bf16[16,128]{1,0:T(8,128)(2,1)}, u32[]{:S(2)}) copy-start(bf16[16,128]{1,0:T(8,128)(2,1)} %ab.1) | copy-start | bytes 12292
  101.1 14.9 %all-to-all-start.2 = ((bf16[32,16,128]{2,1,0:T(8,128)(2,1)}), bf16[32,16,128]{2,1,0:T(8,128)(2,1)S(1)}, u32[]{:S(2)}, u32[]{:S(2)}) async-start(bf16[32,16,128]{2,1,0:T(8,128)(2,1)} %get-tuple-element.32), calls=%async_computation.2 | async-start | bytes 262144 | tf_op jit(solution)/shard_map/all_to_all | solution.py:332
  116.9 22.7 %all-to-all-start.3 = ((bf16[16,16,384]{2,1,0:T(8,128)(2,1)}), bf16[16,16,384]{2,1,0:T(8,128)(2,1)S(1)}, u32[]{:S(2)}, u32[]{:S(2)}) async-start(bf16[16,16,384]{2,1,0:T(8,128)(2,1)} %shard_map.133), calls=%async_computation.3 | async-start | bytes 393216 | tf_op jit(solution)/shard_map/all_to_all | solution.py:337

commit v3 on v2

--- a/solution.py
+++ b/solution.py
@@ -12,7 +12,7 @@
 LOG2E = 1.4426950408889634
 HIDDEN_SCORE = -2e30
 LOWEST = -1e30
-CHUNK = 128
+CHUNK = 256
 DOCS = 4
 VMEM_BYTES = 48 * 1024 * 1024
 bf16 = jnp.bfloat16
@@ -31,23 +31,21 @@
     return lax.dot_general(a, b, (((0,), (0,)), ((), ())), preferred_element_type=f32)
 
 
-def stage(order, q, g, kv, qs, gs, kvs, part):
-    sources, tokens, width = q.shape
-    half = tokens // 2
-    grp = width // HEAD_DIM
-    for t in range(2):
-        for i in range(sources):
-            for n in range(grp):
-                at = (i * grp + n) * half
-                span = slice(n * HEAD_DIM, (n + 1) * HEAD_DIM)
-                qs[t, at : at + half, :] = q[i, t * half : (t + 1) * half, span]
-                gs[t, at : at + half, :] = g[i, t * half : (t + 1) * half, span]
+def sort_keys(order, kv, kvs, part):
     for b in range(kv.shape[0] // part):
         to = pl.multiple_of(order[b] * part, part)
         kvs[pl.ds(to, part), :] = kv[b * part : (b + 1) * part, :]
 
 
-def block_rows(order, outer, docs, t, part):
+def stacked(qg, t, half, which):
+    sources, _, width = qg.shape
+    rows = slice((2 * which + t) * half, (2 * which + t + 1) * half)
+    return jnp.concatenate(
+        [qg[i, rows, n : n + HEAD_DIM] for i in range(sources) for n in range(0, width, HEAD_DIM)], axis=0
+    )
+
+
+def block_rows(outer, order, docs, t, part):
     half = docs.shape[1]
     block = order[2 * outer[0] + t]
     own = docs[pl.ds(block, 1), :]
@@ -72,28 +70,28 @@
     return jnp.concatenate([bias] * heads, axis=1)
 
 
-def forward_kernel(part, inner, outer, order, docs, q, g, kv, lows, stats, low, qs, gs, kvs):
-    stage(order, q, g, kv, qs, gs, kvs, part)
-    columns = qs.shape[1]
-    heads = columns // docs.shape[1]
+def forward_kernel(part, inner, outer, order, docs, qg, kv, stats, low, kvs):
+    sort_keys(order, kv, kvs, part)
+    both = [block_rows(outer, order, docs, t, part) for t in range(2)]
+    half = docs.shape[1]
+    columns = stats.shape[-1] // 2
+    heads = columns // half
     stats[...] = jnp.zeros_like(stats)
-    whole = lows[0].astype(f32)
-    for i in range(1, lows.shape[0]):
-        whole = whole + lows[i].astype(f32)
-    half = docs.shape[1]
-    shift = (half - part * inner[0]) % half
-    mine = [pltpu.roll(whole[:, t * half : (t + 1) * half], shift, 1)[:, :part] for t in range(2)]
-    low[...] = jnp.concatenate(mine, axis=1)
+    rank, rows = low.shape
+    total_low = qg[0, qg.shape[1] - rank :, :HEAD_DIM].astype(f32)
+    for i in range(1, qg.shape[0]):
+        total_low = total_low + qg[i, qg.shape[1] - rank :, :HEAD_DIM].astype(f32)
+    low[...] = total_low[:, :rows]
     for t in range(2):
-        places, first, low_chunk, high = block_rows(order, outer, docs, t, part)
+        places, first, low_chunk, high = both[t]
 
         def body(c, carried, t=t, places=places, first=first):
             peak, total, dot = carried
             at = pl.multiple_of(c * CHUNK, CHUNK)
             k = kvs[pl.ds(at, CHUNK), :HEAD_DIM]
             v = kvs[pl.ds(at, CHUNK), HEAD_DIM:]
-            s = nt(k, qs[t]) * (SCALE * LOG2E) + chunk_bias(inner, places, first, c, part, heads)
-            dp = nt(v, gs[t])
+            s = nt(k, stacked(qg, t, half, 0)) * (SCALE * LOG2E) + chunk_bias(inner, places, first, c, part, heads)
+            dp = nt(v, stacked(qg, t, half, 1))
             new = jnp.maximum(peak, jnp.max(s, axis=0, keepdims=True))
             w = jnp.exp2(s - new)
             factor = jnp.exp2(peak - new)
@@ -120,24 +118,26 @@
     return peak + jnp.log2(total), dot / total
 
 
-def key_kernel(part, inner, outer, order, docs, q, g, kv, stats, dkv, qs, gs, kvs, acc):
-    stage(order, q, g, kv, qs, gs, kvs, part)
-    columns = qs.shape[1]
-    heads = columns // docs.shape[1]
+def key_kernel(part, inner, outer, order, docs, qg, kv, stats, dkv, kvs, acc):
+    sort_keys(order, kv, kvs, part)
+    both = [block_rows(outer, order, docs, t, part) for t in range(2)]
+    half = docs.shape[1]
+    columns = stats.shape[-1] // 2
+    heads = columns // half
     acc[...] = jnp.zeros_like(acc)
     for t in range(2):
-        places, first, low_chunk, high = block_rows(order, outer, docs, t, part)
+        places, first, low_chunk, high = both[t]
         lse, delta = row_terms(stats, t, columns)
 
         def body(c, carried, t=t, places=places, first=first, lse=lse, delta=delta):
             at = pl.multiple_of(c * CHUNK, CHUNK)
             k = kvs[pl.ds(at, CHUNK), :HEAD_DIM]
             v = kvs[pl.ds(at, CHUNK), HEAD_DIM:]
-            s = nt(k, qs[t]) * (SCALE * LOG2E) + chunk_bias(inner, places, first, c, part, heads)
+            s = nt(k, stacked(qg, t, half, 0)) * (SCALE * LOG2E) + chunk_bias(inner, places, first, c, part, heads)
             p = jnp.exp2(s - lse)
-            ds = (p * (nt(v, gs[t]) - delta)).astype(bf16)
-            acc[pl.ds(at, CHUNK), :HEAD_DIM] += nn(ds, qs[t])
-            acc[pl.ds(at, CHUNK), HEAD_DIM:] += nn(p.astype(bf16), gs[t])
+            ds = (p * (nt(v, stacked(qg, t, half, 1)) - delta)).astype(bf16)
+            acc[pl.ds(at, CHUNK), :HEAD_DIM] += nn(ds, stacked(qg, t, half, 0))
+            acc[pl.ds(at, CHUNK), HEAD_DIM:] += nn(p.astype(bf16), stacked(qg, t, half, 1))
             return carried
 
         lax.fori_loop(low_chunk, high, body, 0)
@@ -147,14 +147,15 @@
             dkv[z, t * part : (t + 1) * part, :] = acc[pl.ds(at, part), :].astype(bf16)
 
 
-def query_kernel(part, inner, outer, order, docs, q, g, kv, stats, dq, qs, gs, kvs, dqt):
-    stage(order, q, g, kv, qs, gs, kvs, part)
-    columns = qs.shape[1]
+def query_kernel(part, inner, outer, order, docs, qg, kv, stats, dq, kvs, dqt):
+    sort_keys(order, kv, kvs, part)
+    both = [block_rows(outer, order, docs, t, part) for t in range(2)]
     half = docs.shape[1]
+    columns = stats.shape[-1] // 2
     heads = columns // half
     grp = heads // stats.shape[0]
     for t in range(2):
-        places, first, low_chunk, high = block_rows(order, outer, docs, t, part)
+        places, first, low_chunk, high = both[t]
         lse, delta = row_terms(stats, t, columns)
         dqt[...] = jnp.zeros_like(dqt)
 
@@ -162,8 +163,8 @@
             at = pl.multiple_of(c * CHUNK, CHUNK)
             k = kvs[pl.ds(at, CHUNK), :HEAD_DIM]
             v = kvs[pl.ds(at, CHUNK), HEAD_DIM:]
-            s = nt(k, qs[t]) * (SCALE * LOG2E) + chunk_bias(inner, places, first, c, part, heads)
-            dqt[...] += tn(k, (jnp.exp2(s - lse) * (nt(v, gs[t]) - delta)).astype(bf16))
+            s = nt(k, stacked(qg, t, half, 0)) * (SCALE * LOG2E) + chunk_bias(inner, places, first, c, part, heads)
+            dqt[...] += tn(k, (jnp.exp2(s - lse) * (nt(v, stacked(qg, t, half, 1)) - delta)).astype(bf16))
             return carried
 
         lax.fori_loop(low_chunk, high, body, 0)
@@ -174,24 +175,40 @@
             )
 
 
-def spread_kernel(part, inner, keys, values, kv, held, arrived):
-    half = keys.shape[0] // 2
-    copies = []
+def input_kernel(
+    part, inner, hidden_, at_, queries, grad_out, keys, values, qg, kv, hidden, at, low, wide, mixed, arrived
+):
+    sources, _, width = qg.shape
+    tokens = queries.shape[0]
+    half = tokens // 2
+    pairs = [(queries, wide.at[:tokens, :]), (grad_out, wide.at[tokens:, :]), (hidden_, hidden), (at_, at)]
     for t in range(2):
         here = pl.multiple_of(t * half + inner[0] * part, part)
-        for n, source in enumerate((keys, values)):
-            copy = pltpu.make_async_copy(
-                source.at[pl.ds(here, part), :],
-                held.at[t * part : (t + 1) * part, n * HEAD_DIM : (n + 1) * HEAD_DIM],
-                arrived.at[2 * t + n],
-            )
-            copy.start()
-            copies.append(copy)
+        to = slice(t * part, (t + 1) * part)
+        pairs += [(keys.at[pl.ds(here, part), :], mixed.at[to, :HEAD_DIM])]
+        pairs += [(values.at[pl.ds(here, part), :], mixed.at[to, HEAD_DIM:])]
+    copies = [pltpu.make_async_copy(source, target, arrived.at[n]) for n, (source, target) in enumerate(pairs)]
+    for copy in copies:
+        copy.start()
     for copy in copies:
         copy.wait()
-    whole = held[...]
-    for o in range(kv.shape[0]):
-        kv[o] = whole
+    pairs = [(wide, qg.at[i, : 2 * tokens, :]) for i in range(sources)] + [(mixed, kv)]
+    last = [
+        pltpu.make_async_copy(source, target, arrived.at[len(copies) + n]) for n, (source, target) in enumerate(pairs)
+    ]
+    for copy in last:
+        copy.start()
+    whole = nt(at[...], hidden[...])
+    empty = jnp.zeros((whole.shape[0], width - 2 * part), f32)
+    for i in range(sources):
+        mine = [whole[:, t * half + i * part : t * half + (i + 1) * part] for t in range(2)]
+        low[i] = jnp.concatenate(mine + [empty], axis=1).astype(bf16)
+    for i in range(sources):
+        copy = pltpu.make_async_copy(low.at[i], qg.at[i, 2 * tokens :, :], arrived.at[len(copies) + len(pairs) + i])
+        copy.start()
+        last.append(copy)
+    for copy in last:
+        copy.wait()
 
 
 def home_kernel(parts, ab, low, dkv, payload):
@@ -240,7 +257,7 @@
     gb[...] = total[:, width:]
 
 
-def call(kernel, out_shape, specs, scratch=(), cost=None, vmem=VMEM_BYTES):
+def call(kernel, out_shape, specs, scratch=(), cost=None, vmem=VMEM_BYTES, outs=None):
     spaces = {"s": pltpu.SMEM, "v": pltpu.VMEM, "h": pltpu.HBM}
     single = not isinstance(out_shape, tuple)
     return pl.pallas_call(
@@ -249,7 +266,7 @@
         in_specs=[pl.BlockSpec(memory_space=spaces[s]) for s in specs],
         out_specs=pl.BlockSpec(memory_space=pltpu.VMEM)
         if single
-        else tuple(pl.BlockSpec(memory_space=pltpu.VMEM) for _ in out_shape),
+        else tuple(pl.BlockSpec(memory_space=spaces[o]) for o in outs or "v" * len(out_shape)),
         scratch_shapes=list(scratch),
         compiler_params=pltpu.CompilerParams(vmem_limit_bytes=vmem),
         cost_estimate=cost,
@@ -270,51 +287,56 @@
     rank = adapter_b.shape[0]
 
     width = hidden_in.shape[1]
-    ids = (inner.astype(jnp.int32)[None], outer.astype(jnp.int32)[None])
     docs = doc_ids.reshape(-1, half)
-    kv = call(
-        functools.partial(spread_kernel, part),
-        sd((n_outer, rows, 2 * HEAD_DIM), bf16),
-        "shh",
-        [pltpu.VMEM((rows, 2 * HEAD_DIM), bf16), pltpu.SemaphoreType.DMA((4,))],
+    ids = (inner.astype(jnp.int32)[None], outer.astype(jnp.int32)[None], block_order)
+    qg, kv = call(
+        functools.partial(input_kernel, part),
+        (
+            sd((n_inner, 2 * tokens + rank, queries.shape[1]), bf16),
+            sd((rows, 2 * HEAD_DIM), bf16),
+        ),
+        "shhhhhh",
+        [
+            pltpu.VMEM(hidden_in.shape, bf16),
+            pltpu.VMEM((rank, width), bf16),
+            pltpu.VMEM((n_inner, rank, queries.shape[1]), bf16),
+            pltpu.VMEM((2 * tokens, queries.shape[1]), bf16),
+            pltpu.VMEM((rows, 2 * HEAD_DIM), bf16),
+            pltpu.SemaphoreType.DMA((9 + 2 * n_inner,)),
+        ],
         vmem=None,
-    )(ids[0], keys, values)
-    kv = lax.all_to_all(kv, "outer", 0, 0, tiled=True)
-    q = lax.all_gather(queries, "inner", axis=0, tiled=False)
-    g = lax.all_gather(grad_out, "inner", axis=0, tiled=False)
-    lows = lax.all_gather(nt(adapter_a.T, hidden_in).astype(bf16), "inner", axis=0, tiled=False)
-    kv, q, g, lows = lax.optimization_barrier((kv, q, g, lows))
-    kv = kv.reshape(total_rows, 2 * HEAD_DIM)
+        outs="hh",
+    )(ids[0], hidden_in, adapter_a.T, queries, grad_out, keys, values)
+    qg = lax.all_to_all(qg, "inner", 0, 0, tiled=True)
+    kv = lax.all_gather(kv, "outer", axis=0, tiled=True)
 
     staged = [
-        pltpu.VMEM((2, columns, HEAD_DIM), bf16),
-        pltpu.VMEM((2, columns, HEAD_DIM), bf16),
         pltpu.VMEM((total_rows, 2 * HEAD_DIM), bf16),
     ]
     pair = 2 * columns * total_rows * HEAD_DIM
     stats, low = call(
         functools.partial(forward_kernel, part),
         (sd((4, 2 * columns), f32), sd((rank, rows), f32)),
-        "sssvvvvv",
+        "sssvvv",
         staged,
         pl.CostEstimate(flops=2 * pair, bytes_accessed=2 << 20, transcendentals=columns * total_rows),
-    )(*ids, block_order, docs, q, g, kv, lows)
+    )(*ids, docs, qg, kv)
     stats = lax.all_gather(stats, "inner", axis=0, tiled=False)
     dkv = call(
         functools.partial(key_kernel, part),
         sd((n_outer, rows, 2 * HEAD_DIM), bf16),
-        "sssvvvvv",
+        "sssvvvv",
         staged + [pltpu.VMEM((total_rows, 2 * HEAD_DIM), f32)],
         pl.CostEstimate(flops=4 * pair, bytes_accessed=3 << 20, transcendentals=columns * total_rows),
-    )(*ids, block_order, docs, q, g, kv, stats)
+    )(*ids, docs, qg, kv, stats)
     dkv, stats = lax.optimization_barrier((dkv, stats))
     dq = call(
         functools.partial(query_kernel, part),
         sd((n_inner, tokens, queries.shape[1]), bf16),
-        "sssvvvvv",
+        "sssvvvv",
         staged + [pltpu.VMEM((HEAD_DIM, columns), f32)],
         pl.CostEstimate(flops=3 * pair, bytes_accessed=3 << 20, transcendentals=columns * total_rows),
-    )(*ids, block_order, docs, q, g, kv, stats)
+    )(*ids, docs, qg, kv, stats)
 
     home = lax.all_to_all(dkv, "outer", 0, 0, tiled=True)
     own = lax.dynamic_index_in_dim(dq, inner, 0, keepdims=False).astype(f32)

time: 141 us -> 140 us (level); the launches traced: 140 us -> 138 us
  blocking collectives: 38.8 us -> 50.6 us
  starting transfers between devices: 49 us -> 37.9 us
  waiting for transfers between devices: 36.8 us -> 32.6 us
  Pallas kernels: 12.6 us -> 14.5 us
    all_gather x3 -> x1, blocking collectives: 24.5 us -> 36.2 us  [on_device(): kv = lax.all_gather(kv, 'outer', axis=0, tiled=True)]
    all_to_all x1, starting transfers between devices: 15.4 us -> 4.44 us  [on_device(): qg = lax.all_to_all(qg, 'inner', 0, 0, tiled=True)]
    all_to_all x1, waiting for transfers between devices: 3.52 us -> 0.01 us  [on_device(): qg = lax.all_to_all(qg, 'inner', 0, 0, tiled=True)]
  transfers between devices with their start and end apart: 7 -> 7, of which waited for: 6 -> 5; matrix products, arithmetic and copies ran while one was open for 1% -> 1% of each run, Pallas kernels for 2% -> 2%
where the time goes in v3:
time: 140 us; the launch traced here: 138 us
  blocking collectives  50.6 us (36%)
  starting transfers between devices  37.9 us (27%)
  waiting for transfers between devices  32.6 us (23%)
  Pallas kernels  14.5 us (10%)
    all_gather x1, blocking collectives, on_device(): kv = lax.all_gather(kv, 'outer', axis=0, tiled=True)  36.2 us
    all_to_all x1, waiting for transfers between devices, on_device(): payload = lax.all_to_all(payload, 'outer', 0, 0, tiled=True)  15.9 us
    all_to_all x1, starting transfers between devices, on_device(): home = lax.all_to_all(dkv, 'outer', 0, 0, tiled=True)  10.3 us
    all_to_all x1, waiting for transfers between devices, on_device(): home = lax.all_to_all(dkv, 'outer', 0, 0, tiled=True)  9.61 us
    ppermute x3, starting transfers between devices, on_device(): lax.ppermute(sent, 'inner', [(i, i ^ d) for i in range(n_inner)])  9.37 us
    all_to_all x1, starting transfers between devices, on_device(): payload = lax.all_to_all(payload, ('head', 'inner'), 0, 0, tiled=True)  7.66 us
    all_gather x1, blocking collectives, on_device(): dkv = lax.all_gather(dkv, 'inner', axis=0, tiled=True)  7.32 us
    all_gather x1, blocking collectives, on_device(): stats = lax.all_gather(stats, 'inner', axis=0, tiled=False)  7.03 us
  transfers between devices with their start and end apart: 7, of which 5 were waited for; matrix products, arithmetic and copies ran while one was open for 1% of the time, Pallas kernels for 2%

profile of v3, /device:TPU:32, one launch (start us, length us, event | category | flops | bytes accessed | tf_op | source)
XLA Modules:
  0.0 137.8 jit_solution(989188303451059370)
XLA Ops:
  0.6 2.2 %shard_map.128 = (bf16[4,528,256]{2,1,0:T(8,128)(2,1)}, bf16[64,256]{1,0:T(8,128)(2,1)}) custom-call(s32[1]{0:T(128)} %bitcast.inner, bf16[256,256]{1,0:T(8,128)(2,1)} %hidden.1, bf16[16,256]{1,0:T(8,128)(2,1)} %bitcast.25, bf16[256,256]{1,0:T(8,128)(2,1)} %queries.1, bf16[256,256]{1,0:T(8,128)(2,1)} %grad_out.1, bf16[256,128]{1,0:T(8,128)(2,1)} %keys.1, ...), custom_call_target="tpu_custom_call" | custom-call | tf_op jit(solution)/shard_map/pallas_call | solution.py:292
  2.9 4.4 %all-to-all-start = ((bf16[4,528,256]{2,1,0:T(8,128)(2,1)}), bf16[4,528,256]{2,1,0:T(8,128)(2,1)S(1)}, u32[]{:S(2)}, u32[]{:S(2)}) async-start(bf16[4,528,256]{2,1,0:T(8,128)(2,1)} %get-tuple-element.21), calls=%async_computation | async-start | bytes 2162688 | tf_op jit(solution)/shard_map/all_to_all | solution.py:310
  7.3 36.2 %all_gather.12.kv = bf16[1024,256]{1,0:T(8,128)(2,1)S(1)} all-gather(bf16[64,256]{1,0:T(8,128)(2,1)S(1)} %copy-done.4), channel_id=1, replica_groups=mesh['head'=8,'outer'=16,'inner'=4] {'outer'}, dimensions={0}, use_global_device_ids=true | all-gather | bytes 557056 | tf_op jit(solution)/shard_map/all_gather | solution.py:311
  43.6 2.5 %shard_map.129 = (f32[4,2048]{1,0:T(4,128)S(1)}, f32[16,64]{1,0:T(8,128)S(1)}) custom-call(s32[1]{0:T(128)} %bitcast.inner, s32[1]{0:T(128)} %bitcast.1.outer, s32[32]{0:T(128)S(1)} %copy-done.3, s32[32,128]{1,0:T(8,128)S(1)} %bitcast.21, bf16[4,528,256]{2,1,0:T(8,128)(2,1)S(1)} %all-to-all-done.qg, bf16[1024,256]{1,0:T(8,128)(2,1)S(1)} %all_gather.12.kv), custom_call_target="tpu_custom_call" | custom-call | flops 536870912 | bytes 2097152 | tf_op jit(solution)/shard_map/pallas_call | solution.py:317
  46.1 7.0 %all-gather.1.stats = f32[4,4,2048]{2,1,0:T(4,128)S(1)} all-gather(f32[1,4,2048]{2,1,0:T(4,128)S(1)} %bitcast.20), channel_id=2, replica_groups=mesh['head'=8,'outer'=16,'inner'=4] {'inner'}, dimensions={0}, use_global_device_ids=true | all-gather | bytes 163840 | tf_op jit(solution)/shard_map/all_gather | solution.py:324
  53.1 4.3 %shard_map.130 = bf16[16,64,256]{2,1,0:T(8,128)(2,1)} custom-call(s32[1]{0:T(128)} %bitcast.inner, s32[1]{0:T(128)} %bitcast.1.outer, s32[32]{0:T(128)S(1)} %copy-done.3, s32[32,128]{1,0:T(8,128)S(1)} %bitcast.22, bf16[4,528,256]{2,1,0:T(8,128)(2,1)S(1)} %all-to-all-done.qg, bf16[1024,256]{1,0:T(8,128)(2,1)S(1)} %all_gather.12.kv, ...), custom_call_target="tpu_custom_call" | custom-call | flops 1073741824 | bytes 3145728 | tf_op jit(solution)/shard_map/pallas_call | solution.py:325
  57.4 10.3 %all-to-all-start.1 = ((bf16[16,64,256]{2,1,0:T(8,128)(2,1)}), bf16[16,64,256]{2,1,0:T(8,128)(2,1)S(1)}, u32[]{:S(2)}, u32[]{:S(2)}) async-start(bf16[16,64,256]{2,1,0:T(8,128)(2,1)} %shard_map.130), calls=%async_computation.1 | async-start | bytes 1048576 | tf_op jit(solution)/shard_map/all_to_all | solution.py:341
  67.7 3.1 %shard_map.131 = bf16[4,256,256]{2,1,0:T(8,128)(2,1)S(1)} custom-call(s32[1]{0:T(128)} %bitcast.inner, s32[1]{0:T(128)} %bitcast.1.outer, s32[32]{0:T(128)S(1)} %copy-done.3, s32[32,128]{1,0:T(8,128)S(1)} %bitcast.23, bf16[4,528,256]{2,1,0:T(8,128)(2,1)S(1)} %all-to-all-done.qg, bf16[1024,256]{1,0:T(8,128)(2,1)S(1)} %all_gather.12.kv, ...), custom_call_target="tpu_custom_call" | custom-call | flops 805306368 | bytes 3145728 | tf_op jit(solution)/shard_map/pallas_call | solution.py:333
  70.9 2.1 %collective-permute-start = (bf16[256,256]{1,0:T(8,128)(2,1)S(1)}, bf16[256,256]{1,0:T(8,128)(2,1)S(1)}, u32[]{:S(2)}, u32[]{:S(2)}) collective-permute-start(bf16[256,256]{1,0:T(8,128)(2,1)S(1)} %get-tuple-element.37), channel_id=1, source_target_pairs={{0,1},{1,0},{2,3},{3,2},{4,5},{5,4},{6,7},{7,6},{8,9},{9,8},{10,11... | collective-permute-start | bytes 393224 | tf_op jit(solution)/shard_map/ppermute | solution.py:345
  73.0 5.3 %collective-permute-start.1 = (bf16[256,256]{1,0:T(8,128)(2,1)S(1)}, bf16[256,256]{1,0:T(8,128)(2,1)S(1)}, u32[]{:S(2)}, u32[]{:S(2)}) collective-permute-start(bf16[256,256]{1,0:T(8,128)(2,1)S(1)} %get-tuple-element.39), channel_id=1, source_target_pairs={{0,2},{1,3},{2,0},{3,1},{4,6},{5,7},{6,4},{7,5},{8,10},{9,11},{10,... | collective-permute-start | bytes 393224 | tf_op jit(solution)/shard_map/ppermute | solution.py:345
  78.3 2.0 %collective-permute-start.2 = (bf16[256,256]{1,0:T(8,128)(2,1)S(1)}, bf16[256,256]{1,0:T(8,128)(2,1)S(1)}, u32[]{:S(2)}, u32[]{:S(2)}) collective-permute-start(bf16[256,256]{1,0:T(8,128)(2,1)S(1)} %get-tuple-element.38), channel_id=1, source_target_pairs={{0,3},{1,2},{2,1},{3,0},{4,7},{5,6},{6,5},{7,4},{8,11},{9,10},{10,... | collective-permute-start | bytes 393224 | tf_op jit(solution)/shard_map/ppermute | solution.py:345
  80.3 2.1 %collective-permute-done.1 = bf16[256,256]{1,0:T(8,128)(2,1)S(1)} collective-permute-done((bf16[256,256]{1,0:T(8,128)(2,1)S(1)}, bf16[256,256]{1,0:T(8,128)(2,1)S(1)}, u32[]{:S(2)}, u32[]{:S(2)}) %collective-permute-start.1) | collective-permute-done | bytes 131104 | tf_op jit(solution)/shard_map/ppermute | solution.py:345
  82.4 4.7 %collective-permute-done.2 = bf16[256,256]{1,0:T(8,128)(2,1)S(1)} collective-permute-done((bf16[256,256]{1,0:T(8,128)(2,1)S(1)}, bf16[256,256]{1,0:T(8,128)(2,1)S(1)}, u32[]{:S(2)}, u32[]{:S(2)}) %collective-permute-start.2) | collective-permute-done | bytes 131104 | tf_op jit(solution)/shard_map/ppermute | solution.py:345
  87.2 0.7 fusion.3
  87.9 9.6 %all-to-all-done.1.parts = bf16[16,64,256]{2,1,0:T(8,128)(2,1)S(1)} async-done(((bf16[16,64,256]{2,1,0:T(8,128)(2,1)}), bf16[16,64,256]{2,1,0:T(8,128)(2,1)S(1)}, u32[]{:S(2)}, u32[]{:S(2)}) %all-to-all-start.1) | async-done | bytes 524320 | tf_op jit(solution)/shard_map/all_to_all | solution.py:341
  97.5 0.8 shard_map.132
  98.4 7.7 %all-to-all-start.2 = ((bf16[32,16,128]{2,1,0:T(8,128)(2,1)}), bf16[32,16,128]{2,1,0:T(8,128)(2,1)S(1)}, u32[]{:S(2)}, u32[]{:S(2)}) async-start(bf16[32,16,128]{2,1,0:T(8,128)(2,1)} %get-tuple-element.28), calls=%async_computation.2 | async-start | bytes 262144 | tf_op jit(solution)/shard_map/all_to_all | solution.py:354
  106.0 7.3 %all_gather.15.dkv = bf16[256,256]{1,0:T(8,128)(2,1)S(1)} all-gather(bf16[64,256]{1,0:T(8,128)(2,1)S(1)} %get-tuple-element.29), channel_id=1, replica_groups=mesh['head'=8,'outer'=16,'inner'=4] {'inner'}, dimensions={0}, use_global_device_ids=true | all-gather | bytes 163840 | tf_op jit(solution)/shard_map/all_gather | solution.py:355
  113.4 0.2 all-to-all-done.2.parts
  113.6 0.9 shard_map.133
  114.5 6.1 %all-to-all-start.3 = ((bf16[16,16,384]{2,1,0:T(8,128)(2,1)}), bf16[16,16,384]{2,1,0:T(8,128)(2,1)S(1)}, u32[]{:S(2)}, u32[]{:S(2)}) async-start(bf16[16,16,384]{2,1,0:T(8,128)(2,1)} %shard_map.133), calls=%async_computation.3 | async-start | bytes 393216 | tf_op jit(solution)/shard_map/all_to_all | solution.py:359
  120.6 0.7 fusion.4
  121.3 15.9 %all-to-all-done.3.parts = bf16[16,16,384]{2,1,0:T(8,128)(2,1)S(1)} async-done(((bf16[16,16,384]{2,1,0:T(8,128)(2,1)}), bf16[16,16,384]{2,1,0:T(8,128)(2,1)S(1)}, u32[]{:S(2)}, u32[]{:S(2)}) %all-to-all-start.3) | async-done | bytes 196640 | tf_op jit(solution)/shard_map/all_to_all | solution.py:359
  137.2 0.6 shard_map.134
  (14 shorter events, 0.1 us)
Async XLA Ops:
  2.8 4.5 %copy-start.4 = (bf16[64,256]{1,0:T(8,128)(2,1)S(1)}, bf16[64,256]{1,0:T(8,128)(2,1)}, u32[]{:S(2)}) copy-start(bf16[64,256]{1,0:T(8,128)(2,1)} %get-tuple-element.22) | copy-start | bytes 98308
  2.9 40.7 %copy-start.2 = (s32[4096]{0:T(1024)S(1)}, s32[4096]{0:T(1024)}, u32[]{:S(2)}) copy-start(s32[4096]{0:T(1024)} %param.17) | copy-start | bytes 49156
  2.9 40.7 %copy-start.3 = (s32[32]{0:T(128)S(1)}, s32[32]{0:T(128)}, u32[]{:S(2)}) copy-start(s32[32]{0:T(128)} %order.5) | copy-start | bytes 388
  2.9 40.7 %all-to-all-start = ((bf16[4,528,256]{2,1,0:T(8,128)(2,1)}), bf16[4,528,256]{2,1,0:T(8,128)(2,1)S(1)}, u32[]{:S(2)}, u32[]{:S(2)}) async-start(bf16[4,528,256]{2,1,0:T(8,128)(2,1)} %get-tuple-element.21), calls=%async_computation | async-start | bytes 2162688 | tf_op jit(solution)/shard_map/all_to_all | solution.py:310
  57.4 40.1 %all-to-all-start.1 = ((bf16[16,64,256]{2,1,0:T(8,128)(2,1)}), bf16[16,64,256]{2,1,0:T(8,128)(2,1)S(1)}, u32[]{:S(2)}, u32[]{:S(2)}) async-start(bf16[16,64,256]{2,1,0:T(8,128)(2,1)} %shard_map.130), calls=%async_computation.1 | async-start | bytes 1048576 | tf_op jit(solution)/shard_map/all_to_all | solution.py:341
  70.9 26.7 %copy-start.1 = (bf16[16,128]{1,0:T(8,128)(2,1)S(1)}, bf16[16,128]{1,0:T(8,128)(2,1)}, u32[]{:S(2)}) copy-start(bf16[16,128]{1,0:T(8,128)(2,1)} %ab.1) | copy-start | bytes 12292
  70.9 42.7 %copy-start = (bf16[256,256]{1,0:T(8,128)(2,1)S(1)}, bf16[256,256]{1,0:T(8,128)(2,1)}, u32[]{:S(2)}) copy-start(bf16[256,256]{1,0:T(8,128)(2,1)} %hidden.1) | copy-start | bytes 393220
  70.9 9.4 %collective-permute-start = (bf16[256,256]{1,0:T(8,128)(2,1)S(1)}, bf16[256,256]{1,0:T(8,128)(2,1)S(1)}, u32[]{:S(2)}, u32[]{:S(2)}) collective-permute-start(bf16[256,256]{1,0:T(8,128)(2,1)S(1)} %get-tuple-element.37), channel_id=1, source_target_pairs={{0,1},{1,0},{2,3},{3,2},{4,5},{5,4},{6,7},{7,6},{8,9},{9,8},{10,11... | collective-permute-start | bytes 393224 | tf_op jit(solution)/shard_map/ppermute | solution.py:345
  73.0 9.4 %collective-permute-start.1 = (bf16[256,256]{1,0:T(8,128)(2,1)S(1)}, bf16[256,256]{1,0:T(8,128)(2,1)S(1)}, u32[]{:S(2)}, u32[]{:S(2)}) collective-permute-start(bf16[256,256]{1,0:T(8,128)(2,1)S(1)} %get-tuple-element.39), channel_id=1, source_target_pairs={{0,2},{1,3},{2,0},{3,1},{4,6},{5,7},{6,4},{7,5},{8,10},{9,11},{10,... | collective-permute-start | bytes 393224 | tf_op jit(solution)/shard_map/ppermute | solution.py:345
  78.3 8.9 %collective-permute-start.2 = (bf16[256,256]{1,0:T(8,128)(2,1)S(1)}, bf16[256,256]{1,0:T(8,128)(2,1)S(1)}, u32[]{:S(2)}, u32[]{:S(2)}) collective-permute-start(bf16[256,256]{1,0:T(8,128)(2,1)S(1)} %get-tuple-element.38), channel_id=1, source_target_pairs={{0,3},{1,2},{2,1},{3,0},{4,7},{5,6},{6,5},{7,4},{8,11},{9,10},{10,... | collective-permute-start | bytes 393224 | tf_op jit(solution)/shard_map/ppermute | solution.py:345
  98.4 15.2 %all-to-all-start.2 = ((bf16[32,16,128]{2,1,0:T(8,128)(2,1)}), bf16[32,16,128]{2,1,0:T(8,128)(2,1)S(1)}, u32[]{:S(2)}, u32[]{:S(2)}) async-start(bf16[32,16,128]{2,1,0:T(8,128)(2,1)} %get-tuple-element.28), calls=%async_computation.2 | async-start | bytes 262144 | tf_op jit(solution)/shard_map/all_to_all | solution.py:354
  114.5 22.7 %all-to-all-start.3 = ((bf16[16,16,384]{2,1,0:T(8,128)(2,1)}), bf16[16,16,384]{2,1,0:T(8,128)(2,1)S(1)}, u32[]{:S(2)}, u32[]{:S(2)}) async-start(bf16[16,16,384]{2,1,0:T(8,128)(2,1)} %shard_map.133), calls=%async_computation.3 | async-start | bytes 393216 | tf_op jit(solution)/shard_map/all_to_all | solution.py:359

commit v4 on v3

--- a/solution.py
+++ b/solution.py
@@ -61,11 +61,11 @@
     return places, first, low, high
 
 
-def chunk_bias(inner, places, first, c, part, heads):
+def chunk_bias(inner, places, first, c, used, part, heads):
     half = places.shape[1]
     n = c * CHUNK + lax.broadcasted_iota(jnp.int32, (CHUNK, half), 0)
     keys = (n // part) * half + part * inner[0] + n % part
-    seen = (keys <= places) & (keys >= first)
+    seen = (keys <= jnp.where(used, places, -1)) & (keys >= first)
     bias = jnp.where(seen, 0.0, HIDDEN_SCORE)
     return jnp.concatenate([bias] * heads, axis=1)
 
@@ -82,29 +82,34 @@
     for i in range(1, qg.shape[0]):
         total_low = total_low + qg[i, qg.shape[1] - rank :, :HEAD_DIM].astype(f32)
     low[...] = total_low[:, :rows]
-    for t in range(2):
-        places, first, low_chunk, high = both[t]
-
-        def body(c, carried, t=t, places=places, first=first):
-            peak, total, dot = carried
+    steps = jnp.maximum(both[0][3] - both[0][2], both[1][3] - both[1][2])
+
+    def body(n, carried):
+        out = []
+        for t in range(2):
+            places, first, low_chunk, high = both[t]
+            peak, total, dot = carried[t]
+            used = low_chunk + n < high
+            c = jnp.minimum(low_chunk + n, high - 1)
             at = pl.multiple_of(c * CHUNK, CHUNK)
             k = kvs[pl.ds(at, CHUNK), :HEAD_DIM]
             v = kvs[pl.ds(at, CHUNK), HEAD_DIM:]
-            s = nt(k, stacked(qg, t, half, 0)) * (SCALE * LOG2E) + chunk_bias(inner, places, first, c, part, heads)
+            bias = chunk_bias(inner, places, first, c, used, part, heads)
+            s = nt(k, stacked(qg, t, half, 0)) * (SCALE * LOG2E) + bias
             dp = nt(v, stacked(qg, t, half, 1))
             new = jnp.maximum(peak, jnp.max(s, axis=0, keepdims=True))
             w = jnp.exp2(s - new)
             factor = jnp.exp2(peak - new)
             total = total * factor + jnp.sum(w, axis=0, keepdims=True)
             dot = dot * factor + jnp.sum(w * dp, axis=0, keepdims=True)
-            return new, total, dot
-
-        zero = jnp.zeros((1, columns), f32)
-        peak, total, dot = lax.fori_loop(low_chunk, high, body, (zero + LOWEST, zero, zero))
-        span = slice(t * columns, (t + 1) * columns)
-        stats[0:1, span] = peak
-        stats[1:2, span] = total
-        stats[2:3, span] = dot
+            out.append((new, total, dot))
+        return tuple(out)
+
+    zero = jnp.zeros((1, columns), f32)
+    found = lax.fori_loop(0, steps, body, ((zero + LOWEST, zero, zero),) * 2)
+    for t in range(2):
+        for row, value in enumerate(found[t]):
+            stats[row : row + 1, t * columns : (t + 1) * columns] = value
 
 
 def row_terms(stats, t, columns):
@@ -125,22 +130,31 @@
     columns = stats.shape[-1] // 2
     heads = columns // half
     acc[...] = jnp.zeros_like(acc)
-    for t in range(2):
-        places, first, low_chunk, high = both[t]
-        lse, delta = row_terms(stats, t, columns)
-
-        def body(c, carried, t=t, places=places, first=first, lse=lse, delta=delta):
+    terms = [row_terms(stats, t, columns) for t in range(2)]
+    steps = jnp.maximum(both[0][3] - both[0][2], both[1][3] - both[1][2])
+
+    def body(n, carried):
+        found = []
+        for t in range(2):
+            places, first, low_chunk, high = both[t]
+            lse, delta = terms[t]
+            used = low_chunk + n < high
+            c = jnp.minimum(low_chunk + n, high - 1)
             at = pl.multiple_of(c * CHUNK, CHUNK)
             k = kvs[pl.ds(at, CHUNK), :HEAD_DIM]
             v = kvs[pl.ds(at, CHUNK), HEAD_DIM:]
-            s = nt(k, stacked(qg, t, half, 0)) * (SCALE * LOG2E) + chunk_bias(inner, places, first, c, part, heads)
-            p = jnp.exp2(s - lse)
-            ds = (p * (nt(v, stacked(qg, t, half, 1)) - delta)).astype(bf16)
-            acc[pl.ds(at, CHUNK), :HEAD_DIM] += nn(ds, stacked(qg, t, half, 0))
-            acc[pl.ds(at, CHUNK), HEAD_DIM:] += nn(p.astype(bf16), stacked(qg, t, half, 1))
-            return carried
-
-        lax.fori_loop(low_chunk, high, body, 0)
+            bias = chunk_bias(inner, places, first, c, used, part, heads)
+            q = stacked(qg, t, half, 0)
+            g = stacked(qg, t, half, 1)
+            p = jnp.exp2(nt(k, q) * (SCALE * LOG2E) + bias - lse)
+            ds = (p * (nt(v, g) - delta)).astype(bf16)
+            found.append((at, nn(ds, q), nn(p.astype(bf16), g)))
+        for at, dk, dv in found:
+            acc[pl.ds(at, CHUNK), :HEAD_DIM] += dk
+            acc[pl.ds(at, CHUNK), HEAD_DIM:] += dv
+        return carried
+
+    lax.fori_loop(0, steps, body, 0)
     for z in range(dkv.shape[0]):
         for t in range(2):
             at = pl.multiple_of(order[2 * z + t] * part, part)
@@ -163,7 +177,7 @@
             at = pl.multiple_of(c * CHUNK, CHUNK)
             k = kvs[pl.ds(at, CHUNK), :HEAD_DIM]
             v = kvs[pl.ds(at, CHUNK), HEAD_DIM:]
-            s = nt(k, stacked(qg, t, half, 0)) * (SCALE * LOG2E) + chunk_bias(inner, places, first, c, part, heads)
+            s = nt(k, stacked(qg, t, half, 0)) * (SCALE * LOG2E) + chunk_bias(inner, places, first, c, True, part, heads)
             dqt[...] += tn(k, (jnp.exp2(s - lse) * (nt(v, stacked(qg, t, half, 1)) - delta)).astype(bf16))
             return carried
 
@@ -190,14 +204,19 @@
     copies = [pltpu.make_async_copy(source, target, arrived.at[n]) for n, (source, target) in enumerate(pairs)]
     for copy in copies:
         copy.start()
-    for copy in copies:
-        copy.wait()
     pairs = [(wide, qg.at[i, : 2 * tokens, :]) for i in range(sources)] + [(mixed, kv)]
     last = [
         pltpu.make_async_copy(source, target, arrived.at[len(copies) + n]) for n, (source, target) in enumerate(pairs)
     ]
-    for copy in last:
+    for copy in copies[:2]:
+        copy.wait()
+    for copy in last[:-1]:
         copy.start()
+    for copy in copies[4:]:
+        copy.wait()
+    last[-1].start()
+    for copy in copies[2:4]:
+        copy.wait()
     whole = nt(at[...], hidden[...])
     empty = jnp.zeros((whole.shape[0], width - 2 * part), f32)
     for i in range(sources):

time: 140 us -> 138 us (0.986); the launches traced: 138 us -> 138 us
  Pallas kernels: 14.5 us -> 16.1 us
  transfers between devices with their start and end apart: 7 -> 7, of which waited for: 5 -> 5; matrix products, arithmetic and copies ran while one was open for 1% -> 1% of each run, Pallas kernels for 2% -> 3%
where the time goes in v4:
time: 138 us
  blocking collectives  50.6 us (37%)
  starting transfers between devices  37.5 us (27%)
  waiting for transfers between devices  31.9 us (23%)
  Pallas kernels  16.1 us (12%)
    all_gather x1, blocking collectives, on_device(): kv = lax.all_gather(kv, 'outer', axis=0, tiled=True)  36.2 us
    all_to_all x1, waiting for transfers between devices, on_device(): payload = lax.all_to_all(payload, 'outer', 0, 0, tiled=True)  15.9 us
    all_to_all x1, starting transfers between devices, on_device(): home = lax.all_to_all(dkv, 'outer', 0, 0, tiled=True)  9.93 us
    ppermute x3, starting transfers between devices, on_device(): lax.ppermute(sent, 'inner', [(i, i ^ d) for i in range(n_inner)])  9.37 us
    all_to_all x1, waiting for transfers between devices, on_device(): home = lax.all_to_all(dkv, 'outer', 0, 0, tiled=True)  8.96 us
    all_to_all x1, starting transfers between devices, on_device(): payload = lax.all_to_all(payload, ('head', 'inner'), 0, 0, tiled=True)  7.65 us
    all_gather x1, blocking collectives, on_device(): dkv = lax.all_gather(dkv, 'inner', axis=0, tiled=True)  7.32 us
    all_gather x1, blocking collectives, on_device(): stats = lax.all_gather(stats, 'inner', axis=0, tiled=False)  7.03 us
  transfers between devices with their start and end apart: 7, of which 5 were waited for; matrix products, arithmetic and copies ran while one was open for 1% of the time, Pallas kernels for 3%

profile of v4, /device:TPU:32, one launch (start us, length us, event | category | flops | bytes accessed | tf_op | source)
XLA Modules:
  0.0 138.4 jit_solution(6434581591942335978)
XLA Ops:
  0.6 2.1 %shard_map.128 = (bf16[4,528,256]{2,1,0:T(8,128)(2,1)}, bf16[64,256]{1,0:T(8,128)(2,1)}) custom-call(s32[1]{0:T(128)} %bitcast.inner, bf16[256,256]{1,0:T(8,128)(2,1)} %hidden.1, bf16[16,256]{1,0:T(8,128)(2,1)} %bitcast.25, bf16[256,256]{1,0:T(8,128)(2,1)} %queries.1, bf16[256,256]{1,0:T(8,128)(2,1)} %grad_out.1, bf16[256,128]{1,0:T(8,128)(2,1)} %keys.1, ...), custom_call_target="tpu_custom_call" | custom-call | tf_op jit(solution)/shard_map/pallas_call | solution.py:311
  2.8 4.4 %all-to-all-start = ((bf16[4,528,256]{2,1,0:T(8,128)(2,1)}), bf16[4,528,256]{2,1,0:T(8,128)(2,1)S(1)}, u32[]{:S(2)}, u32[]{:S(2)}) async-start(bf16[4,528,256]{2,1,0:T(8,128)(2,1)} %get-tuple-element.21), calls=%async_computation | async-start | bytes 2162688 | tf_op jit(solution)/shard_map/all_to_all | solution.py:329
  7.3 36.2 %all_gather.12.kv = bf16[1024,256]{1,0:T(8,128)(2,1)S(1)} all-gather(bf16[64,256]{1,0:T(8,128)(2,1)S(1)} %copy-done.4), channel_id=1, replica_groups=mesh['head'=8,'outer'=16,'inner'=4] {'outer'}, dimensions={0}, use_global_device_ids=true | all-gather | bytes 557056 | tf_op jit(solution)/shard_map/all_gather | solution.py:330
  43.5 3.0 %shard_map.129 = (f32[4,2048]{1,0:T(4,128)S(1)}, f32[16,64]{1,0:T(8,128)S(1)}) custom-call(s32[1]{0:T(128)} %bitcast.inner, s32[1]{0:T(128)} %bitcast.1.outer, s32[32]{0:T(128)S(1)} %copy-done.3, s32[32,128]{1,0:T(8,128)S(1)} %bitcast.21, bf16[4,528,256]{2,1,0:T(8,128)(2,1)S(1)} %all-to-all-done.qg, bf16[1024,256]{1,0:T(8,128)(2,1)S(1)} %all_gather.12.kv), custom_call_target="tpu_custom_call" | custom-call | flops 536870912 | bytes 2097152 | tf_op jit(solution)/shard_map/pallas_call | solution.py:336
  46.4 7.0 %all-gather.1.stats = f32[4,4,2048]{2,1,0:T(4,128)S(1)} all-gather(f32[1,4,2048]{2,1,0:T(4,128)S(1)} %bitcast.20), channel_id=2, replica_groups=mesh['head'=8,'outer'=16,'inner'=4] {'inner'}, dimensions={0}, use_global_device_ids=true | all-gather | bytes 163840 | tf_op jit(solution)/shard_map/all_gather | solution.py:343
  53.5 4.9 %shard_map.130 = bf16[16,64,256]{2,1,0:T(8,128)(2,1)} custom-call(s32[1]{0:T(128)} %bitcast.inner, s32[1]{0:T(128)} %bitcast.1.outer, s32[32]{0:T(128)S(1)} %copy-done.3, s32[32,128]{1,0:T(8,128)S(1)} %bitcast.22, bf16[4,528,256]{2,1,0:T(8,128)(2,1)S(1)} %all-to-all-done.qg, bf16[1024,256]{1,0:T(8,128)(2,1)S(1)} %all_gather.12.kv, ...), custom_call_target="tpu_custom_call" | custom-call | flops 1073741824 | bytes 3145728 | tf_op jit(solution)/shard_map/pallas_call | solution.py:344
  58.4 9.9 %all-to-all-start.1 = ((bf16[16,64,256]{2,1,0:T(8,128)(2,1)}), bf16[16,64,256]{2,1,0:T(8,128)(2,1)S(1)}, u32[]{:S(2)}, u32[]{:S(2)}) async-start(bf16[16,64,256]{2,1,0:T(8,128)(2,1)} %shard_map.130), calls=%async_computation.1 | async-start | bytes 1048576 | tf_op jit(solution)/shard_map/all_to_all | solution.py:360
  68.3 3.8 %shard_map.131 = bf16[4,256,256]{2,1,0:T(8,128)(2,1)S(1)} custom-call(s32[1]{0:T(128)} %bitcast.inner, s32[1]{0:T(128)} %bitcast.1.outer, s32[32]{0:T(128)S(1)} %copy-done.3, s32[32,128]{1,0:T(8,128)S(1)} %bitcast.23, bf16[4,528,256]{2,1,0:T(8,128)(2,1)S(1)} %all-to-all-done.qg, bf16[1024,256]{1,0:T(8,128)(2,1)S(1)} %all_gather.12.kv, ...), custom_call_target="tpu_custom_call" | custom-call | flops 805306368 | bytes 3145728 | tf_op jit(solution)/shard_map/pallas_call | solution.py:352
  72.2 2.1 %collective-permute-start = (bf16[256,256]{1,0:T(8,128)(2,1)S(1)}, bf16[256,256]{1,0:T(8,128)(2,1)S(1)}, u32[]{:S(2)}, u32[]{:S(2)}) collective-permute-start(bf16[256,256]{1,0:T(8,128)(2,1)S(1)} %get-tuple-element.37), channel_id=1, source_target_pairs={{0,1},{1,0},{2,3},{3,2},{4,5},{5,4},{6,7},{7,6},{8,9},{9,8},{10,11... | collective-permute-start | bytes 393224 | tf_op jit(solution)/shard_map/ppermute | solution.py:364
  74.2 5.3 %collective-permute-start.1 = (bf16[256,256]{1,0:T(8,128)(2,1)S(1)}, bf16[256,256]{1,0:T(8,128)(2,1)S(1)}, u32[]{:S(2)}, u32[]{:S(2)}) collective-permute-start(bf16[256,256]{1,0:T(8,128)(2,1)S(1)} %get-tuple-element.39), channel_id=1, source_target_pairs={{0,2},{1,3},{2,0},{3,1},{4,6},{5,7},{6,4},{7,5},{8,10},{9,11},{10,... | collective-permute-start | bytes 393224 | tf_op jit(solution)/shard_map/ppermute | solution.py:364
  79.5 2.0 %collective-permute-start.2 = (bf16[256,256]{1,0:T(8,128)(2,1)S(1)}, bf16[256,256]{1,0:T(8,128)(2,1)S(1)}, u32[]{:S(2)}, u32[]{:S(2)}) collective-permute-start(bf16[256,256]{1,0:T(8,128)(2,1)S(1)} %get-tuple-element.38), channel_id=1, source_target_pairs={{0,3},{1,2},{2,1},{3,0},{4,7},{5,6},{6,5},{7,4},{8,11},{9,10},{10,... | collective-permute-start | bytes 393224 | tf_op jit(solution)/shard_map/ppermute | solution.py:364
  81.6 2.1 %collective-permute-done.1 = bf16[256,256]{1,0:T(8,128)(2,1)S(1)} collective-permute-done((bf16[256,256]{1,0:T(8,128)(2,1)S(1)}, bf16[256,256]{1,0:T(8,128)(2,1)S(1)}, u32[]{:S(2)}, u32[]{:S(2)}) %collective-permute-start.1) | collective-permute-done | bytes 131104 | tf_op jit(solution)/shard_map/ppermute | solution.py:364
  83.7 4.7 %collective-permute-done.2 = bf16[256,256]{1,0:T(8,128)(2,1)S(1)} collective-permute-done((bf16[256,256]{1,0:T(8,128)(2,1)S(1)}, bf16[256,256]{1,0:T(8,128)(2,1)S(1)}, u32[]{:S(2)}, u32[]{:S(2)}) %collective-permute-start.2) | collective-permute-done | bytes 131104 | tf_op jit(solution)/shard_map/ppermute | solution.py:364
  88.4 0.7 fusion.3
  89.1 9.0 %all-to-all-done.1.parts = bf16[16,64,256]{2,1,0:T(8,128)(2,1)S(1)} async-done(((bf16[16,64,256]{2,1,0:T(8,128)(2,1)}), bf16[16,64,256]{2,1,0:T(8,128)(2,1)S(1)}, u32[]{:S(2)}, u32[]{:S(2)}) %all-to-all-start.1) | async-done | bytes 524320 | tf_op jit(solution)/shard_map/all_to_all | solution.py:360
  98.1 0.8 shard_map.132
  98.9 7.7 %all-to-all-start.2 = ((bf16[32,16,128]{2,1,0:T(8,128)(2,1)}), bf16[32,16,128]{2,1,0:T(8,128)(2,1)S(1)}, u32[]{:S(2)}, u32[]{:S(2)}) async-start(bf16[32,16,128]{2,1,0:T(8,128)(2,1)} %get-tuple-element.28), calls=%async_computation.2 | async-start | bytes 262144 | tf_op jit(solution)/shard_map/all_to_all | solution.py:373
  106.6 7.3 %all_gather.15.dkv = bf16[256,256]{1,0:T(8,128)(2,1)S(1)} all-gather(bf16[64,256]{1,0:T(8,128)(2,1)S(1)} %get-tuple-element.29), channel_id=1, replica_groups=mesh['head'=8,'outer'=16,'inner'=4] {'inner'}, dimensions={0}, use_global_device_ids=true | all-gather | bytes 163840 | tf_op jit(solution)/shard_map/all_gather | solution.py:374
  113.9 0.2 all-to-all-done.2.parts
  114.1 0.9 shard_map.133
  115.0 6.1 %all-to-all-start.3 = ((bf16[16,16,384]{2,1,0:T(8,128)(2,1)}), bf16[16,16,384]{2,1,0:T(8,128)(2,1)S(1)}, u32[]{:S(2)}, u32[]{:S(2)}) async-start(bf16[16,16,384]{2,1,0:T(8,128)(2,1)} %shard_map.133), calls=%async_computation.3 | async-start | bytes 393216 | tf_op jit(solution)/shard_map/all_to_all | solution.py:378
  121.2 0.7 fusion.4
  121.8 15.9 %all-to-all-done.3.parts = bf16[16,16,384]{2,1,0:T(8,128)(2,1)S(1)} async-done(((bf16[16,16,384]{2,1,0:T(8,128)(2,1)}), bf16[16,16,384]{2,1,0:T(8,128)(2,1)S(1)}, u32[]{:S(2)}, u32[]{:S(2)}) %all-to-all-start.3) | async-done | bytes 196640 | tf_op jit(solution)/shard_map/all_to_all | solution.py:378
  137.7 0.6 shard_map.134
  (14 shorter events, 0.1 us)
Async XLA Ops:
  2.8 4.5 %copy-start.4 = (bf16[64,256]{1,0:T(8,128)(2,1)S(1)}, bf16[64,256]{1,0:T(8,128)(2,1)}, u32[]{:S(2)}) copy-start(bf16[64,256]{1,0:T(8,128)(2,1)} %get-tuple-element.22) | copy-start | bytes 98308
  2.8 40.7 %copy-start.2 = (s32[4096]{0:T(1024)S(1)}, s32[4096]{0:T(1024)}, u32[]{:S(2)}) copy-start(s32[4096]{0:T(1024)} %param.17) | copy-start | bytes 49156
  2.8 40.7 %copy-start.3 = (s32[32]{0:T(128)S(1)}, s32[32]{0:T(128)}, u32[]{:S(2)}) copy-start(s32[32]{0:T(128)} %order.5) | copy-start | bytes 388
  2.8 40.7 %all-to-all-start = ((bf16[4,528,256]{2,1,0:T(8,128)(2,1)}), bf16[4,528,256]{2,1,0:T(8,128)(2,1)S(1)}, u32[]{:S(2)}, u32[]{:S(2)}) async-start(bf16[4,528,256]{2,1,0:T(8,128)(2,1)} %get-tuple-element.21), calls=%async_computation | async-start | bytes 2162688 | tf_op jit(solution)/shard_map/all_to_all | solution.py:329
  58.4 39.7 %all-to-all-start.1 = ((bf16[16,64,256]{2,1,0:T(8,128)(2,1)}), bf16[16,64,256]{2,1,0:T(8,128)(2,1)S(1)}, u32[]{:S(2)}, u32[]{:S(2)}) async-start(bf16[16,64,256]{2,1,0:T(8,128)(2,1)} %shard_map.130), calls=%async_computation.1 | async-start | bytes 1048576 | tf_op jit(solution)/shard_map/all_to_all | solution.py:360
  72.1 26.0 %copy-start.1 = (bf16[16,128]{1,0:T(8,128)(2,1)S(1)}, bf16[16,128]{1,0:T(8,128)(2,1)}, u32[]{:S(2)}) copy-start(bf16[16,128]{1,0:T(8,128)(2,1)} %ab.1) | copy-start | bytes 12292
  72.1 42.1 %copy-start = (bf16[256,256]{1,0:T(8,128)(2,1)S(1)}, bf16[256,256]{1,0:T(8,128)(2,1)}, u32[]{:S(2)}) copy-start(bf16[256,256]{1,0:T(8,128)(2,1)} %hidden.1) | copy-start | bytes 393220
  72.2 9.4 %collective-permute-start = (bf16[256,256]{1,0:T(8,128)(2,1)S(1)}, bf16[256,256]{1,0:T(8,128)(2,1)S(1)}, u32[]{:S(2)}, u32[]{:S(2)}) collective-permute-start(bf16[256,256]{1,0:T(8,128)(2,1)S(1)} %get-tuple-element.37), channel_id=1, source_target_pairs={{0,1},{1,0},{2,3},{3,2},{4,5},{5,4},{6,7},{7,6},{8,9},{9,8},{10,11... | collective-permute-start | bytes 393224 | tf_op jit(solution)/shard_map/ppermute | solution.py:364
  74.2 9.4 %collective-permute-start.1 = (bf16[256,256]{1,0:T(8,128)(2,1)S(1)}, bf16[256,256]{1,0:T(8,128)(2,1)S(1)}, u32[]{:S(2)}, u32[]{:S(2)}) collective-permute-start(bf16[256,256]{1,0:T(8,128)(2,1)S(1)} %get-tuple-element.39), channel_id=1, source_target_pairs={{0,2},{1,3},{2,0},{3,1},{4,6},{5,7},{6,4},{7,5},{8,10},{9,11},{10,... | collective-permute-start | bytes 393224 | tf_op jit(solution)/shard_map/ppermute | solution.py:364
  79.5 8.9 %collective-permute-start.2 = (bf16[256,256]{1,0:T(8,128)(2,1)S(1)}, bf16[256,256]{1,0:T(8,128)(2,1)S(1)}, u32[]{:S(2)}, u32[]{:S(2)}) collective-permute-start(bf16[256,256]{1,0:T(8,128)(2,1)S(1)} %get-tuple-element.38), channel_id=1, source_target_pairs={{0,3},{1,2},{2,1},{3,0},{4,7},{5,6},{6,5},{7,4},{8,11},{9,10},{10,... | collective-permute-start | bytes 393224 | tf_op jit(solution)/shard_map/ppermute | solution.py:364
  98.9 15.2 %all-to-all-start.2 = ((bf16[32,16,128]{2,1,0:T(8,128)(2,1)}), bf16[32,16,128]{2,1,0:T(8,128)(2,1)S(1)}, u32[]{:S(2)}, u32[]{:S(2)}) async-start(bf16[32,16,128]{2,1,0:T(8,128)(2,1)} %get-tuple-element.28), calls=%async_computation.2 | async-start | bytes 262144 | tf_op jit(solution)/shard_map/all_to_all | solution.py:373
  115.0 22.7 %all-to-all-start.3 = ((bf16[16,16,384]{2,1,0:T(8,128)(2,1)}), bf16[16,16,384]{2,1,0:T(8,128)(2,1)S(1)}, u32[]{:S(2)}, u32[]{:S(2)}) async-start(bf16[16,16,384]{2,1,0:T(8,128)(2,1)} %shard_map.133), calls=%async_computation.3 | async-start | bytes 393216 | tf_op jit(solution)/shard_map/all_to_all | solution.py:378
